TPU v7x, 32 devices: a whole 2x2x4 slice. The times are simulated.
32 devices in a mesh: seq: 8 (over z, y), head: 4 (over x, core).
Axes of the slice: x: 2, y: 2, z: 4, core: 2. Of those that a mesh axis runs over, the one named last changes fastest.
Arguments:
- mamba_inner: bfloat16 [1024, 3072], P('seq', 'head'), may hold values from -6 to 6
- mamba_groups: bfloat16 [1024, 512], P('seq'), may hold values from -6 to 6
- selective_gate: bfloat16 [1024, 3072], P('seq', 'head'), may hold values from -6 to 6
- step_raw: float32 [48, 1024], P('head', 'seq'), may hold values from -3 to 3
- step_bias: float32 [48], P('head'), may hold values from -0.5 to 0.5
- decay_log: float32 [48], P('head'), may hold values from -12 to -2
- conv_inner: float32 [4, 3072], P(None, 'head'), may hold values from -3 to 3
- conv_groups: float32 [4, 512], replicated, may hold values from -3 to 3
- gated_norm_gain: float32 [3072], P('head'), may hold values from 0.1 to 1.9
- query_rows: bfloat16 [1024, 1024], P('seq', 'head'), may hold values from -8 to 8
- key_rows: bfloat16 [1024, 256], P('seq'), may hold values from -8 to 8
- value_rows: bfloat16 [1024, 256], P('seq'), may hold values from -6 to 6
- segment_ids: int32 [1024], P('seq'), may hold values from 0 to 15, never falling along the last dimension, each value on 1 to 682 neighbouring positions
- mamba_proj: bfloat16 [3072, 2048], P('head'), may hold values from -0.109375 to 0.109375
- attn_proj: bfloat16 [1024, 2048], P('head'), may hold values from -0.1875 to 0.1875
Outputs:
- mixed: bfloat16 [1024, 2048], P('seq', 'head')
Inputs may be any that keep to these rules, and one draw needn't show every extreme that they name: `segment_ids`: prompt numbers never fall along the tokens; each prompt holds 1 to 682 tokens and one holds exactly 682.
All inputs are finite; a program needn't handle non-finite values.
Results may differ from a plain program's by a relative error of at most 0.015.
Values may be sent and summed in bfloat16 or wider, within the bound.
A program may use at most 128 MiB of HBM per device.

v0:
```python
import math

import jax
import jax.numpy as jnp
from jax import lax
from jax.sharding import PartitionSpec as P

HEAD_CHANNELS = 64
STATE_SIZE = 256
QH = 8
KVH = 2
HD = 128


def shifted(value, axis, steps):
    count = lax.axis_size(axis)
    first, last = (max(0, -steps), min(count, count - steps))
    return lax.ppermute(value, axis, [(source, source + steps) for source in range(first, last)])


def entering(array, axis, combine, identity):
    length, position = (lax.axis_size(axis), lax.axis_index(axis))
    everything = jax.tree.map(
        lambda part, kind: lax.all_gather(part.astype(kind), axis),
        array,
        (jnp.bfloat16, jnp.bfloat16),
    )
    start = jax.tree.map(
        lambda part, zero: jnp.broadcast_to(jnp.asarray(zero, part.dtype), part.shape),
        array,
        identity,
    )

    def turn(k, before):
        reached = k < position
        new = combine(
            before, jax.tree.map(lambda part, own: part[k].astype(own.dtype), everything, array)
        )
        return jax.tree.map(lambda a, b: jnp.where(reached, a, b), new, before)

    return lax.fori_loop(0, length, turn, start)


def conv_silu(rows, weight, segs, rim_rows, rim_segs):
    item_count = rows.shape[0]
    padded = jnp.concatenate([rim_rows.astype(jnp.float32), rows.astype(jnp.float32)], 0)
    seg_pad = jnp.concatenate([rim_segs, segs], 0)
    total = jnp.zeros(rows.shape, jnp.float32)
    for offset in range(weight.shape[0]):
        window = padded[offset : offset + item_count]
        keep = (seg_pad[offset : offset + item_count] == segs).astype(jnp.float32)
        total = total + weight[offset][None, :] * window * keep[:, None]
    return jax.nn.silu(total).astype(jnp.bfloat16)


def mamba_local(inner, groups, segs, steps, rates, prev_last):
    highest = lax.Precision.HIGHEST
    cumul = jnp.cumsum(-steps * rates[:, None], axis=1)
    read_b = groups[:, :STATE_SIZE]
    read_c = groups[:, STATE_SIZE:]
    intersection = jnp.dot(read_c, read_b.T, preferred_element_type=jnp.float32)
    order = jnp.arange(segs.shape[0], dtype=jnp.int32)
    live = (segs[:, None] == segs[None, :]) & (order[:, None] >= order[None, :])
    decays = jnp.exp(jnp.where(live[None], cumul[:, :, None] - cumul[:, None, :], -jnp.inf))
    mixing = intersection[None] * decays
    scaled = inner.astype(jnp.float32) * steps.T[:, :, None]
    output = jnp.einsum("htj,jhd->thd", mixing, scaled, precision=highest)
    tail = jnp.exp(cumul[:, -1:] - cumul) * (segs == segs[-1]).astype(jnp.float32)[None, :]
    local_state = jnp.einsum(
        "ht,thd,tn->hdn", tail, scaled, read_b.astype(jnp.float32), precision=highest
    )
    through = jnp.exp(cumul[:, -1]) * (segs[-1] == prev_last).astype(jnp.float32)
    return (output, through, local_state, cumul)


def mamba_incoming(output, incoming, groups, segs, cumul, prev_last):
    read_c = groups[:, STATE_SIZE:].astype(jnp.float32)
    joined = (segs == prev_last).astype(jnp.float32)
    from_carry = jnp.einsum("hdn,tn->thd", incoming, read_c, precision=lax.Precision.HIGHEST)
    return output + jnp.exp(cumul).T[:, :, None] * joined[:, None, None] * from_carry


def combine_states(earlier, later):
    return (earlier[0] * later[0], later[0][:, None, None] * earlier[1] + later[1])


def shards(
    mamba_inner,
    mamba_groups,
    selective_gate,
    step_raw,
    step_bias,
    decay_log,
    conv_inner,
    conv_groups,
    gated_norm_gain,
    query_rows,
    key_rows,
    value_rows,
    segment_ids,
    mamba_proj,
    attn_proj,
):
    item_count = segment_ids.shape[0]
    taps = conv_inner.shape[0]
    resident_heads = step_raw.shape[0]
    rim_inner, rim_groups, rim_marks = shifted(
        (
            mamba_inner[item_count - taps + 1 :],
            mamba_groups[item_count - taps + 1 :],
            segment_ids[item_count - taps + 1 :].astype(jnp.bfloat16),
        ),
        "seq",
        1,
    )
    rim_segs = rim_marks.astype(jnp.float32).astype(jnp.int32)
    prev_last = rim_segs[-1]
    inner_filtered = conv_silu(mamba_inner, conv_inner, segment_ids, rim_inner, rim_segs).reshape(
        item_count, resident_heads, HEAD_CHANNELS
    )
    groups_conv = conv_silu(mamba_groups, conv_groups, segment_ids, rim_groups, rim_segs)
    steps = jax.nn.softplus(step_raw + step_bias[:, None])
    rates = jnp.exp(decay_log)
    output, through, local_state, cumul = mamba_local(
        inner_filtered, groups_conv, segment_ids, steps, rates, prev_last
    )
    identity = (jnp.ones_like(through), jnp.zeros_like(local_state))
    carry_decay, carry_state = entering((through, local_state), "seq", combine_states, identity)
    selective_output = mamba_incoming(
        output, carry_state, groups_conv, segment_ids, cumul, prev_last
    )
    gated_values = selective_output * jax.nn.silu(selective_gate.astype(jnp.float32)).reshape(
        item_count, resident_heads, HEAD_CHANNELS
    )
    mean_square = jnp.mean(gated_values * gated_values, axis=-1, keepdims=True)
    normalized_rows = (
        (
            gated_values
            * lax.rsqrt(mean_square + 1e-05)
            * gated_norm_gain.reshape(resident_heads, HEAD_CHANNELS)
        )
        .astype(jnp.bfloat16)
        .reshape(item_count, resident_heads * HEAD_CHANNELS)
    )
    heads_here = query_rows.shape[1] // HD
    group_size = QH // KVH
    kv_index = lax.axis_index("head") * heads_here // group_size
    my_keys = lax.dynamic_slice_in_dim(key_rows, kv_index * HD, HD, 1)
    my_values = lax.dynamic_slice_in_dim(value_rows, kv_index * HD, HD, 1)
    marks = segment_ids.astype(jnp.bfloat16)
    block_start = lax.axis_index("seq") * item_count
    query_pos = block_start + jnp.arange(item_count, dtype=jnp.int32)
    queries = query_rows.reshape(item_count, heads_here, HD).transpose(1, 0, 2)
    scale = 1.0 / math.sqrt(HD)
    start_state = (
        jnp.full((heads_here, item_count), -1e30, jnp.float32),
        jnp.zeros((heads_here, item_count), jnp.float32),
        jnp.zeros((heads_here, item_count, HD), jnp.float32),
    )
    piece_keys = lax.all_gather(my_keys, "seq", axis=0, tiled=True)
    piece_values = lax.all_gather(my_values, "seq", axis=0, tiled=True)
    piece_marks = lax.all_gather(marks, "seq", axis=0, tiled=True)
    rows = piece_keys.shape[0]
    width = math.gcd(rows, item_count)
    blocks = rows // width

    def one_block(state, item):
        top, total, summed = state
        block_keys, block_values, block_marks, offset = item
        key_pos = offset * width + jnp.arange(width, dtype=jnp.int32)
        key_seg = block_marks.astype(jnp.float32).astype(jnp.int32)
        allowed = (
            (key_seg[None, :] == segment_ids[:, None])
            & (key_pos[None, :] <= query_pos[:, None])
            & (key_pos[None, :] >= 0)
        )
        scores = (
            jnp.einsum("hqd,kd->hqk", queries, block_keys, preferred_element_type=jnp.float32)
            * scale
        )
        scores = jnp.where(allowed[None], scores, -jnp.inf)
        new_top = jnp.maximum(top, jnp.max(scores, axis=-1))
        rescale = jnp.exp(top - new_top)
        weights = jnp.exp(scores - new_top[..., None])
        total = total * rescale + jnp.sum(weights, axis=-1)
        summed = summed * rescale[..., None] + jnp.einsum(
            "hqk,kd->hqd",
            weights.astype(jnp.bfloat16),
            block_values,
            preferred_element_type=jnp.float32,
        )
        return ((new_top, total, summed), None)

    items = (
        piece_keys.reshape(blocks, width, HD),
        piece_values.reshape(blocks, width, HD),
        piece_marks.reshape(blocks, width),
        jnp.arange(blocks, dtype=jnp.int32),
    )
    result, unused = lax.scan(one_block, start_state, items)
    top_final, total_final, summed_final = result
    attended = (
        (summed_final / total_final[..., None])
        .astype(jnp.bfloat16)
        .transpose(1, 0, 2)
        .reshape(item_count, heads_here * HD)
    )
    terms = jnp.dot(normalized_rows, mamba_proj, preferred_element_type=jnp.float32) + jnp.dot(
        attended, attn_proj, preferred_element_type=jnp.float32
    )
    return lax.psum_scatter(terms.astype(jnp.bfloat16), "head", scatter_dimension=1, tiled=True)


def solution(mesh):
    placed = (
        P("seq", "head"),
        P("seq", None),
        P("seq", "head"),
        P("head", "seq"),
        P("head"),
        P("head"),
        P(None, "head"),
        P(),
        P("head"),
        P("seq", "head"),
        P("seq", None),
        P("seq", None),
        P("seq"),
        P("head", None),
        P("head", None),
    )
    return jax.shard_map(
        shards, mesh=mesh, in_specs=placed, out_specs=P("seq", "head"), check_vma=False
    )
```

profile of v0, /device:TPU:25, one launch (start us, length us, event | category | flops | bytes accessed | tf_op | source)
XLA Modules:
  0.0 240.2 jit_solution(1705443980735956197)
XLA Ops:
  7.9 3.1 %collective-permute-start.1 = (bf16[3]{0:T(256)(128)(2,1)}, bf16[3]{0:T(256)(128)(2,1)}, u32[]{:S(2)}, u32[]{:S(2)}) collective-permute-start(bf16[3]{0:T(256)(128)(2,1)} %slice.85), channel_id=1, source_target_pairs={{0,4},{4,8},{8,12},{12,16},{16,20},{20,24},{24,28},{1,5},{5,9},{9,... | collective-permute-start | bytes 26 | tf_op jit(solution)/shard_map/ppermute | solution.py:18
  11.8 1.9 collective-permute-start.2
  15.3 1.9 collective-permute-start
  26.4 26.6 %all_gather.23 = bf16[1024,128]{1,0:T(8,128)(2,1)} all-gather(bf16[128,128]{1,0:T(8,128)(2,1)S(1)} %constant_dynamic-slice_fusion.2), channel_id=1, replica_groups=mesh['seq'=8,'head'=4] {'seq'}, dimensions={0}, use_global_device_ids=true | all-gather | bytes 294912 | tf_op jit(solution)/shard_map/all_gather | solution.py:160
  53.7 26.4 %all_gather.24 = bf16[1024,128]{1,0:T(8,128)(2,1)} all-gather(bf16[128,128]{1,0:T(8,128)(2,1)S(1)} %constant_dynamic-slice_fusion.1), channel_id=1, replica_groups=mesh['seq'=8,'head'=4] {'seq'}, dimensions={0}, use_global_device_ids=true | all-gather | bytes 294912 | tf_op jit(solution)/shard_map/all_gather | solution.py:161
  80.1 12.9 %all-gather.2 = bf16[8,1,128]{2,1,0:T(2,128)(2,1)S(1)} all-gather(bf16[1,1,128]{2,1,0:T(2,128)(2,1)S(1)} %get-tuple-element.295), channel_id=1, replica_groups=mesh['seq'=8,'head'=4] {'seq'}, dimensions={0}, use_global_device_ids=true | all-gather | bytes 2304 | tf_op jit(solution)/shard_map/all_gather | solution.py:162
  96.7 2.0 compare_convert_fusion.4
  102.5 2.5 %multiply_convert_fusion.1 = bf16[128,768]{0,1:T(8,128)(2,1)S(1)} fusion(f32[128,768]{0,1:T(8,128)} %convert_element_type.121, f32[3,768]{0,1:T(8,128)S(1)} %convert_element_type.120, f32[768]{0:T(1024)S(1)} %get-tuple-element.241, f32[128]{0:T(128)S(1)} %get-tuple-element.290, f32[768]{0:T(1024)S(1)} %get-tuple-element.242, f32[128]{0:T(128)S(1)} %get-tuple-element.291, ...), kind=kLoop, calls=%fused_computation.74 | loop fusion | flops 1769472 | bytes 612864 | tf_op jit(solution)/shard_map/convert_element_type | solution.py:53
  107.0 32.5 %while.30 = (s32[]{:T(128)}, f32[2,128]{1,0:T(2,128)S(1)}, f32[2,128]{1,0:T(2,128)S(1)}, f32[2,128,128]{2,1,0:T(8,128)S(1)}, bf16[8,128]{1,0:T(8,128)(2,1)}, /*i...) while((s32[]{:T(128)}, f32[2,128]{1,0:T(2,128)S(1)}, ...), condition=%wide.region_7.8_spmd.clone, body=%wide.region_4.7_spmd.clone.sunk | while | flops 17172484 | bytes 840889 | solution.py:200
  144.2 1.8 convert_multiply_fusion
  146.1 2.5 %fusion.76 = f32[128,2048]{1,0:T(8,128)} fusion(bf16[128,256]{0,1:T(8,128)(2,1)S(1)} %bitcast.93, bf16[256,2048]{1,0:T(8,128)(2,1)} %param.33), kind=kOutput, calls=%fused_computation.132 | convolution fusion | flops 134217728 | bytes 2162688 | tf_op jit(solution)/shard_map/dot_general | solution.py:208
  150.3 15.5 %all-reduce = bf16[96]{0:T(256)(128)(2,1)S(1)} all-reduce(bf16[96]{0:T(256)(128)(2,1)S(1)} %dynamic-update-slice), channel_id=2, replica_groups=mesh['seq'=8,'head'=4] {'seq'}, use_global_device_ids=true, to_apply=%add | all-reduce | flops 96 | bytes 384
  166.0 19.0 %all-gather.5.cloned.1.call-done = bf16[96,64,256]{2,1,0:T(8,128)(2,1)} async-done(((bf16[12,64,256]{2,1,0:T(8,128)(2,1)}), bf16[96,64,256]{2,1,0:T(8,128)(2,1)}) %all-gather.5.cloned.1.call-update) | async-done | bytes 3145744 | tf_op jit(solution)/shard_map/all_gather | solution.py:24
  185.0 18.2 %while.29 = (s32[]{:T(128)}, f32[12,64,256]{2,1,0:T(8,128)}, s32[]{:T(128)}, bf16[8,12]{1,0:T(8,128)(2,1)S(1)}, bf16[8,12,64,256]{3,2,1,0:T(8,128)(2,1)}, /*index=5*/s32[]{:T(128)}, s32[]{:T(128)}) while((s32[]{:T(128)}, f32[12,64,256]{2,1,0:T(8,128)}, s32[]{:T(128)}, bf16[8,12]{1,0:T(8,128)(2,1)S(1)}, ...), condition=%wide.region_2.3_spmd.clone, body=%wide.region_1.2_spmd.clone.sunk | while | flops 983056 | bytes 1966305 | solution.py:41
  185.0 2.1 fusion.92
  187.1 2.3 fusion.92
  189.4 2.3 fusion.92
  191.7 2.3 fusion.92
  194.0 2.3 fusion.92
  196.3 2.3 fusion.92
  198.6 2.3 fusion.92
  200.8 2.3 fusion.92
  204.9 2.8 %multiply_reduce_fusion = (f32[128,12]{0,1:T(8,128)S(1)}, f32[128,12,64]{0,2,1:T(8,128)S(1)}) fusion(f32[128,12,64]{0,2,1:T(8,128)} %bitcast.92, f32[128,12,64]{0,2,1:T(8,128)S(1)} %convolution_multiply_fusion.1, f32[12,128]{1,0:T(8,128)S(1)} %reduce_window_sum.11, f32[128,128]{1,0:T(8,128)S(1)} %fusion.66, pred[128,128]{1,0:T(8,128)(4,1)S(1)} %fusion.64, ...), kind=kOutput, calls=%fused_computation.69 | convolution fusion | flops 152173056 | bytes 1476608 | tf_op jit(solution)/shard_map/htj,jhd->thd/dot_general | solution.py:67
  209.3 24.1 %reduce-scatter.2.cloned.1.call-done = bf16[128,512]{1,0:T(8,128)(2,1)} async-done(((bf16[128,2048]{1,0:T(8,128)(2,1)}), bf16[128,512]{1,0:T(8,128)(2,1)}) %reduce-scatter.2.cloned.1.call-update) | async-done | bytes 131088 | tf_op jit(solution)/shard_map/reduce_scatter | solution.py:211
  (173 shorter events, 58.3 us)
Async XLA Ops:
  6.5 201.3 %copy-start = (bf16[768,2048]{1,0:T(8,128)(2,1)S(1)}, bf16[768,2048]{1,0:T(8,128)(2,1)}, u32[]{:S(2)}) copy-start(bf16[768,2048]{1,0:T(8,128)(2,1)} %param.32) | copy-start | bytes 9437188
  6.5 100.5 %copy-start.5 = (s32[128]{0:T(128)S(1)}, s32[128]{0:T(128)}, u32[]{:S(2)}) copy-start(s32[128]{0:T(128)} %param.31) | copy-start | bytes 1540
  6.5 178.4 %all-gather.5.cloned.1.call-start = ((), (), s32[]{:S(2)}) async-start(), calls=%async_computation.2 | async-start | bytes 3538944 | tf_op jit(solution)/shard_map/all_gather | solution.py:24
  7.9 86.8 %collective-permute-start.1 = (bf16[3]{0:T(256)(128)(2,1)}, bf16[3]{0:T(256)(128)(2,1)}, u32[]{:S(2)}, u32[]{:S(2)}) collective-permute-start(bf16[3]{0:T(256)(128)(2,1)} %slice.85), channel_id=1, source_target_pairs={{0,4},{4,8},{8,12},{12,16},{16,20},{20,24},{24,28},{1,5},{5,9},{9,... | collective-permute-start | bytes 26 | tf_op jit(solution)/shard_map/ppermute | solution.py:18
  11.8 87.4 %collective-permute-start.2 = (bf16[3,512]{1,0:T(4,128)(2,1)S(1)}, bf16[3,512]{1,0:T(4,128)(2,1)}, u32[]{:S(2)}, u32[]{:S(2)}) collective-permute-start(bf16[3,512]{1,0:T(4,128)(2,1)S(1)} %slice.95), channel_id=1, source_target_pairs={{0,4},{4,8},{8,12},{12,16},{16,20},{20,24},{24,28},{1,5},{5,9},{9,... | collective-permute-start | bytes 9224 | tf_op jit(solution)/shard_map/ppermute | solution.py:18
  15.3 86.3 %collective-permute-start = (bf16[3,768]{0,1:T(8,128)(2,1)}, bf16[3,768]{0,1:T(8,128)(2,1)}, u32[]{:S(2)}, u32[]{:S(2)}) collective-permute-start(bf16[3,768]{0,1:T(8,128)(2,1)} %copy.27), channel_id=1, source_target_pairs={{0,4},{4,8},{8,12},{12,16},{16,20},{20,24},{24,28},{1,5},{5,9},{9,... | collective-permute-start | bytes 13832 | tf_op jit(solution)/shard_map/ppermute | solution.py:18
  25.2 81.9 %copy-start.6 = (f32[128,12]{0,1:T(8,128)}, f32[128,12]{0,1:T(8,128)S(1)}, u32[]{:S(2)}) copy-start(f32[128,12]{0,1:T(8,128)S(1)} %get-tuple-element.281) | copy-start | bytes 18436
  101.5 3.5 %copy-start.2 = (bf16[128,512]{1,0:T(8,128)(2,1)}, bf16[128,512]{1,0:T(8,128)(2,1)S(1)}, u32[]{:S(2)}) copy-start(bf16[128,512]{1,0:T(8,128)(2,1)S(1)} %multiply_convert_fusion.2) | copy-start | bytes 393220
  105.0 0.7 copy-start.4
  105.0 36.3 %copy-start.10 = (f32[768]{0:T(1024)S(1)}, f32[768]{0:T(1024)}, u32[]{:S(2)}) copy-start(f32[768]{0:T(1024)} %param.27) | copy-start | bytes 9220
  107.0 126.4 %reduce-scatter.2.cloned.1.call-start = ((), (), s32[]{:S(2)}) async-start(), calls=%async_computation.1 | async-start | bytes 655360 | tf_op jit(solution)/shard_map/reduce_scatter | solution.py:211
  139.5 26.4 %copy-start.3 = (bf16[128,512]{1,0:T(8,128)(2,1)S(1)}, bf16[128,512]{1,0:T(8,128)(2,1)}, u32[]{:S(2)}) copy-start(bf16[128,512]{1,0:T(8,128)(2,1)} %copy-done.2) | copy-start | bytes 393220
  185.0 18.2 %copy-start.8 = (f32[128,12]{0,1:T(8,128)S(1)}, f32[128,12]{0,1:T(8,128)}, u32[]{:S(2)}) copy-start(f32[128,12]{0,1:T(8,128)} %get-tuple-element.283) | copy-start | bytes 18436
  185.0 19.9 %copy-start.7 = (f32[128,12]{0,1:T(8,128)S(1)}, f32[128,12]{0,1:T(8,128)}, u32[]{:S(2)}) copy-start(f32[128,12]{0,1:T(8,128)} %copy-done.6) | copy-start | bytes 18436
  185.0 22.7 %copy-start.9 = (f32[12,64]{1,0:T(8,128)S(1)}, f32[12,64]{1,0:T(8,128)}, u32[]{:S(2)}) copy-start(f32[12,64]{1,0:T(8,128)} %mul.345) | copy-start | bytes 9220
  203.1 4.7 %copy-start.1 = (f32[128,2048]{1,0:T(8,128)S(1)}, f32[128,2048]{1,0:T(8,128)}, u32[]{:S(2)}) copy-start(f32[128,2048]{1,0:T(8,128)} %fusion.76) | copy-start | bytes 3145732
Sparse Core Ops, SparseCore 0:
  107.1 77.8 all-gather.4
  209.4 23.9 reduce-scatter.1
where the time goes:
time: 244 us; the launch traced here: 240 us
  blocking collectives  81.4 us (33%)
  waiting for transfers between devices  43.1 us (18%)
  other arithmetic  41.5 us (17%)
  matrix products  25.2 us (10%)
  local copies, waits for them, and re-layouts  21.2 us (9%)
  between operations  15.7 us (6%)
  starting transfers between devices  7 us (3%)
  loops' own time  5.2 us (2%)
    all_gather x1, blocking collectives, shards(): piece_keys = lax.all_gather(my_keys, 'seq', axis=0, tiled=True)  26.6 us
    all_gather x1, blocking collectives, shards(): piece_values = lax.all_gather(my_values, 'seq', axis=0, tiled=True)  26.4 us
    reduce_scatter x1, waiting for transfers between devices, shards(): lax.psum_scatter(terms.astype(jnp.bfloat16), 'head', scatter_dimension=1,...  24.1 us
    all_gather x1, waiting for transfers between devices, entering(): lax.all_gather(part.astype(kind), axis)  19 us
    select_n x8, other arithmetic, turn(): return jax.tree.map(lambda a, b: jnp.where(reached, a, b), new, before)  18.1 us
    unnamed x1, blocking collectives  15.5 us
    all_gather x1, blocking collectives, shards(): piece_marks = lax.all_gather(marks, 'seq', axis=0, tiled=True)  12.9 us
    dot_general x8, matrix products, one_block(): jnp.einsum('hqk,kd->hqd', weights.astype(jnp.bfloat16), block_values, pre...  7.85 us
  transfers between devices with their start and end apart: 5, of which 2 were waited for; matrix products, arithmetic and copies ran while one was open for 24% of the time, Pallas kernels for 0%

commit v1 on v0

v1 whole, which is shorter than its diff:
```python
import functools
import math

import jax
import jax.numpy as jnp
from jax import lax
from jax.experimental import pallas as pl
from jax.experimental.pallas import tpu as pltpu
from jax.sharding import PartitionSpec as P

HEAD_CHANNELS = 64
STATE_SIZE = 256
QH = 8
KVH = 2
HD = 128
LANES = 128
RIM = 16
F32 = jnp.float32
BF16 = jnp.bfloat16
MESH = pl.DeviceIdType.MESH
HIGHEST = lax.Precision.HIGHEST


def dot(a, b, contract, precision=None):
    return lax.dot_general(
        a, b, ((contract[:1], contract[1:]), ((), ())), precision=precision, preferred_element_type=F32
    )


def iota(shape, axis):
    return lax.broadcasted_iota(jnp.int32, shape, axis)


def column(row):
    n = row.shape[1]
    eye = iota((n, n), 0) == iota((n, n), 1)
    return jnp.sum(jnp.where(eye, jnp.broadcast_to(row, (n, n)), 0.0), axis=1, keepdims=True)


def kernel(
    n_seq,
    n_head,
    inner_ref,
    groups_ref,
    gate_ref,
    step_ref,
    bias_ref,
    decay_ref,
    taps_inner_ref,
    taps_groups_ref,
    gain_ref,
    query_ref,
    key_ref,
    value_ref,
    segs_ref,
    mamba_proj_hbm,
    attn_proj_hbm,
    out_ref,
    mproj,
    aproj,
    pad_inner,
    pad_groups,
    rim_inner,
    rim_groups,
    meta,
    kv,
    conv_x,
    conv_bc,
    cumx,
    y_ref,
    state,
    s_send,
    s_recv,
    e_send,
    e_recv,
    f_send,
    f_recv,
    entering,
    both,
    rs_send,
    rs_recv,
    weight_sem,
    rim_sem,
    meta_ss,
    meta_rs,
    kv_ss,
    kv_rs,
    s_ss,
    s_rs,
    e_ss,
    e_rs,
    f_ss,
    f_rs,
    rs_ss,
    rs_rs,
):
    tokens, channels = inner_ref.shape
    heads = step_ref.shape[0]
    half = channels // 2
    chunks = half // LANES
    pairs = channels // LANES
    me = lax.axis_index("seq")
    mine = lax.axis_index("head")
    pair, side = me // 2, me % 2
    last_pair = n_seq // 2 - 1
    heads_here = query_ref.shape[1] // HD

    def at_seq(s):
        return (s, mine)

    def at_head(h):
        return (me, h)

    weights = [
        pltpu.make_async_copy(mamba_proj_hbm, mproj, weight_sem.at[0]),
        pltpu.make_async_copy(attn_proj_hbm, aproj, weight_sem.at[1]),
    ]
    for w in weights:
        w.start()

    barrier = pltpu.get_barrier_semaphore()
    for d in range(1, n_seq):
        pl.semaphore_signal(barrier, inc=1, device_id=at_seq((me + d) % n_seq), device_id_type=MESH)
    for d in range(1, n_head):
        pl.semaphore_signal(barrier, inc=1, device_id=at_head((mine + d) % n_head), device_id_type=MESH)

    kv_head = mine * heads_here // (QH // KVH)
    kv_cols = pl.ds(pl.multiple_of(kv_head * HD, HD), HD)
    kv[me, :, 0:HD] = key_ref[:, kv_cols]
    kv[me, :, HD : 2 * HD] = value_ref[:, kv_cols]

    raw = step_ref[...] + column(bias_ref[...])
    steps = jnp.maximum(raw, 0.0) + jnp.log1p(jnp.exp(-jnp.abs(raw)))
    rates = jnp.exp(column(decay_ref[...]))
    row_t, col_t = iota((tokens, tokens), 0), iota((tokens, tokens), 1)
    upto = (row_t <= col_t).astype(F32)
    cumul = dot(-steps * rates, upto, (1, 0), HIGHEST)
    spread = (iota((heads, channels), 1) // HEAD_CHANNELS == iota((heads, channels), 0)).astype(F32)
    cumx[...] = dot(cumul, spread, (0, 0), HIGHEST)
    stepx = dot(steps, spread, (0, 0), HIGHEST)
    total_row = cumx[tokens - 1 : tokens, :]
    segs_row = segs_ref[...].astype(F32)
    segs_col = column(segs_row)
    last_seg = segs_row[:, tokens - 1 : tokens]
    meta[me, 0:1, :] = total_row
    meta[me, 1:2, 0:tokens] = segs_row
    meta[me, 2:3, :] = jnp.broadcast_to(last_seg, (1, channels))
    pl.semaphore_wait(barrier, n_seq + n_head - 2)

    def rim_copies(target):
        tail = pl.ds(tokens - RIM, RIM)
        return [
            pltpu.make_async_remote_copy(
                src.at[tail, :], dst, rim_sem.at[0, i], rim_sem.at[1, i], device_id=at_seq(target), device_id_type=MESH
            )
            for i, (src, dst) in enumerate(((inner_ref, rim_inner), (groups_ref, rim_groups)))
        ]

    def meta_copy(slot, other):
        return pltpu.make_async_remote_copy(
            meta.at[slot], meta.at[slot], meta_ss.at[other], meta_rs.at[slot], device_id=at_seq(other), device_id_type=MESH
        )

    def kv_copy(slot, other):
        return pltpu.make_async_remote_copy(
            kv.at[slot], kv.at[slot], kv_ss.at[other], kv_rs.at[slot], device_id=at_seq(other), device_id_type=MESH
        )

    following = lax.min(me + 1, n_seq - 1)
    previous = lax.max(me - 1, 0)

    @pl.when(me < n_seq - 1)
    def _():
        for c in rim_copies(following):
            c.start()

    def send_meta(d, _):
        meta_copy(me, (me + d) % n_seq).start()
        return 0

    lax.fori_loop(1, n_seq, send_meta, 0)

    def send_kv(k, _):
        kv_copy(me, k).start()
        return 0

    lax.fori_loop(me + 1, n_seq, send_kv, 0)

    pad_inner[RIM:, :] = inner_ref[...].astype(F32)
    pad_groups[RIM:, :] = groups_ref[...].astype(F32)

    def wait_meta(d, _):
        k = (me + d) % n_seq
        meta_copy(k, k).wait_recv()
        return 0

    lax.fori_loop(1, n_seq, wait_meta, 0)

    @pl.when(me > 0)
    def _():
        for c in rim_copies(previous):
            c.wait_recv()

    @pl.when(me == 0)
    def _():
        rim_inner[...] = jnp.zeros_like(rim_inner)
        rim_groups[...] = jnp.zeros_like(rim_groups)

    pad_inner[0:RIM, :] = rim_inner[...].astype(F32)
    pad_groups[0:RIM, :] = rim_groups[...].astype(F32)

    taps = taps_inner_ref.shape[0]
    prev_last = meta[previous, 2:3, 0:1]
    prev_segs = meta[previous, 1:2, 0:tokens]
    token_col = iota((tokens, 1), 0)
    keeps = []
    for k in range(taps - 1):
        back = taps - 1 - k
        own = jnp.sum(
            jnp.where(row_t - back == col_t, jnp.broadcast_to(segs_row, (tokens, tokens)), 0.0), 1, keepdims=True
        )
        before = jnp.sum(
            jnp.where(row_t - back + tokens == col_t, jnp.broadcast_to(prev_segs, (tokens, tokens)), 0.0),
            1,
            keepdims=True,
        )
        keeps.append(jnp.where(token_col >= back, own, before) == segs_col)

    def conv(pad, weight_ref, out):
        for c in range(0, out.shape[1], LANES):
            cols = slice(c, c + LANES)
            acc = jnp.zeros((tokens, LANES), F32)
            for k in range(taps):
                first = RIM - (taps - 1) + k
                term = weight_ref[k : k + 1, cols] * pad[first : first + tokens, cols]
                acc = acc + (jnp.where(keeps[k], term, 0.0) if k < taps - 1 else term)
            out[:, cols] = jax.nn.silu(acc).astype(BF16)

    conv(pad_groups, taps_groups_ref, conv_bc)
    conv(pad_inner, taps_inner_ref, conv_x)

    read_b = conv_bc[:, :STATE_SIZE]
    read_c = conv_bc[:, STATE_SIZE:]
    in_last = segs_col == last_seg
    tail = jnp.where(in_last, jnp.exp(total_row - cumx[...]), 0.0)
    weighted = (tail * stepx * conv_x[...].astype(F32)).astype(BF16)
    state[...] = dot(read_b, weighted, (0, 0))

    partner = me + 1 - 2 * side
    upper = lax.min(me + 2, n_seq - 1)
    lower = lax.max(me - 2, 0)

    def part(which, c):
        return pl.ds(pl.multiple_of(which * half + c * LANES, LANES), LANES)

    def hop(src, dst, ss, rs, c, target):
        return pltpu.make_async_remote_copy(
            src.at[c], dst.at[c], ss.at[c], rs.at[c], device_id=at_seq(target), device_id_type=MESH
        )

    for c in range(chunks):
        s_send[c] = state[:, part(1 - side, c)].astype(BF16)
        hop(s_send, s_recv, s_ss, s_rs, c, partner).start()

    crossing = dot(read_c, read_b, (1, 1))
    live = (jnp.broadcast_to(segs_row, (tokens, tokens)) == segs_col) & (row_t >= col_t)
    eye = (iota((heads, heads), 0) == iota((heads, heads), 1)).astype(F32)
    cum_cols = dot(cumul, eye, (0, 0), HIGHEST)
    left = iota((tokens, LANES), 1) < HEAD_CHANNELS
    for p in range(pairs):
        got = []
        for h in (2 * p, 2 * p + 1):
            decays = jnp.exp(jnp.where(live, cum_cols[:, h : h + 1] - cumul[h : h + 1, :], -jnp.inf))
            mixing = (crossing * decays * steps[h : h + 1, :]).astype(BF16)
            got.append(dot(mixing, conv_x[:, p * LANES : (p + 1) * LANES], (1, 0)))
        y_ref[:, p * LANES : (p + 1) * LANES] = jnp.where(left, got[0], got[1])

    scale = 1.0 / math.sqrt(HD)
    queries = jnp.concatenate([query_ref[:, h * HD : (h + 1) * HD] for h in range(heads_here)], axis=0)
    rows = heads_here * tokens
    segs_rows = jnp.concatenate([segs_col] * heads_here, axis=0)
    token_rows = jnp.concatenate([token_col] * heads_here, axis=0)

    def attend(d, carry):
        top, total, summed = carry
        k = me - d

        @pl.when(d > 0)
        def _():
            kv_copy(k, k).wait_recv()

        scores = dot(queries, kv[k, :, 0:HD], (1, 1)) * scale
        allowed = (meta[k, 1:2, 0:tokens] == segs_rows) & (
            iota((rows, tokens), 1) + (k - me) * tokens <= token_rows
        )
        scores = jnp.where(allowed, scores, -jnp.inf)
        new_top = jnp.maximum(top, jnp.max(scores, axis=1, keepdims=True))
        rescale = jnp.exp(top - new_top)
        w = jnp.exp(scores - new_top)
        total = total * rescale + jnp.sum(w, axis=1, keepdims=True)
        summed = summed * rescale + dot(w.astype(BF16), kv[k, :, HD : 2 * HD], (1, 0))
        return new_top, total, summed

    top, total, summed = lax.fori_loop(
        0,
        me + 1,
        attend,
        (jnp.full((rows, 1), -1e30, F32), jnp.zeros((rows, 1), F32), jnp.zeros((rows, HD), F32)),
    )
    attended = (summed / total).astype(BF16)
    for h in range(heads_here):
        both[:, channels + h * HD : channels + (h + 1) * HD] = attended[h * tokens : (h + 1) * tokens]

    @pl.when(pair == 0)
    def _():
        e_recv[...] = jnp.zeros_like(e_recv)

    first, second = pair * 2, pair * 2 + 1
    seg_before = meta[lax.max(first - 1, 0), 2:3, 0:LANES]
    seg_first = meta[first, 2:3, 0:LANES]
    seg_second = meta[second, 2:3, 0:LANES]
    on_left = side == 0
    for c in range(chunks):
        cols = part(side, c)
        through_first = jnp.where(seg_first == seg_before, jnp.exp(meta[first, 0:1, cols]), 0.0)
        through_second = jnp.where(seg_second == seg_first, jnp.exp(meta[second, 0:1, cols]), 0.0)
        hop(s_send, s_recv, s_ss, s_rs, c, partner).wait_recv()
        own, others = state[:, cols], s_recv[c].astype(F32)

        @pl.when(pair > 0)
        def _():
            hop(e_send, e_recv, e_ss, e_rs, c, lower).wait_recv()

        enter_first = e_recv[c].astype(F32)
        enter_second = through_first * enter_first + jnp.where(on_left, own, others)

        @pl.when(pair < last_pair)
        def _():
            e_send[c] = (through_second * enter_second + jnp.where(on_left, others, own)).astype(BF16)
            hop(e_send, e_recv, e_ss, e_rs, c, upper).start()

        f_send[c] = jnp.where(on_left, enter_second, enter_first).astype(BF16)
        hop(f_send, f_recv, f_ss, f_rs, c, partner).start()
        entering[:, cols] = jnp.where(on_left, enter_first, enter_second).astype(BF16)

    for c in range(chunks):
        hop(f_send, f_recv, f_ss, f_rs, c, partner).wait_recv()
        entering[:, part(1 - side, c)] = f_recv[c]

    joined = segs_col == prev_last
    same_head = (iota((LANES, LANES), 0) // HEAD_CHANNELS == iota((LANES, LANES), 1) // HEAD_CHANNELS).astype(F32)
    for p in range(pairs):
        cols = slice(p * LANES, (p + 1) * LANES)
        carried = dot(read_c, entering[:, cols], (1, 0))
        y = y_ref[:, cols] + jnp.where(joined, jnp.exp(cumx[:, cols]), 0.0) * carried
        gated = y * jax.nn.silu(gate_ref[:, cols].astype(F32))
        mean_square = dot(gated * gated, same_head, (1, 0), HIGHEST) * (1.0 / HEAD_CHANNELS)
        both[:, cols] = (gated * lax.rsqrt(mean_square + 1e-05) * gain_ref[:, cols]).astype(BF16)

    for w in weights:
        w.wait()
    width = out_ref.shape[1]

    def product(j):
        cols = pl.ds(pl.multiple_of(j * width, LANES), width)
        return dot(both[:, :channels], mproj[:, cols], (1, 0)) + dot(both[:, channels:], aproj[:, cols], (1, 0))

    def rs_copy(d):
        return pltpu.make_async_remote_copy(
            rs_send.at[d - 1],
            rs_recv.at[d - 1],
            rs_ss.at[d - 1],
            rs_rs.at[d - 1],
            device_id=at_head((mine + d) % n_head),
            device_id_type=MESH,
        )

    turns = sorted(range(1, n_head), key=lambda d: abs(d - n_head // 2))
    for d in turns:
        rs_send[d - 1] = product((mine + d) % n_head).astype(BF16)
        rs_copy(d).start()
    result = product(mine)
    for d in turns:
        rs_copy(d).wait_recv()
        result = result + rs_recv[d - 1].astype(F32)
    out_ref[...] = result.astype(BF16)

    for d in turns:
        rs_copy(d).wait_send()

    @pl.when(me < n_seq - 1)
    def _():
        for c in rim_copies(following):
            c.wait_send()

    def sent_meta(d, _):
        meta_copy(me, (me + d) % n_seq).wait_send()
        return 0

    lax.fori_loop(1, n_seq, sent_meta, 0)

    def sent_kv(k, _):
        kv_copy(me, k).wait_send()
        return 0

    lax.fori_loop(me + 1, n_seq, sent_kv, 0)
    for c in range(chunks):
        hop(s_send, s_recv, s_ss, s_rs, c, partner).wait_send()
        hop(f_send, f_recv, f_ss, f_rs, c, partner).wait_send()

        @pl.when(pair < last_pair)
        def _():
            hop(e_send, e_recv, e_ss, e_rs, c, upper).wait_send()


def shards(n_seq, n_head, *arrays):
    (inner, groups, gate, step, bias, decay, taps_i, taps_g, gain, query, key, value, segs, mproj, aproj) = arrays
    tokens, channels = inner.shape
    out_width = mproj.shape[1] // n_head
    chunks = channels // 2 // LANES
    hops = (chunks, STATE_SIZE, LANES)
    vmem = pl.BlockSpec(memory_space=pltpu.VMEM)
    hbm = pl.BlockSpec(memory_space=pl.ANY)
    dma = pltpu.SemaphoreType.DMA
    scratch = [
        pltpu.VMEM(mproj.shape, BF16),
        pltpu.VMEM(aproj.shape, BF16),
        pltpu.VMEM((tokens + RIM, channels), F32),
        pltpu.VMEM((tokens + RIM, groups.shape[1]), F32),
        pltpu.VMEM((RIM, channels), BF16),
        pltpu.VMEM((RIM, groups.shape[1]), BF16),
        pltpu.VMEM((n_seq, 8, channels), F32),
        pltpu.VMEM((n_seq, tokens, 2 * HD), BF16),
        pltpu.VMEM((tokens, channels), BF16),
        pltpu.VMEM((tokens, groups.shape[1]), BF16),
        pltpu.VMEM((tokens, channels), F32),
        pltpu.VMEM((tokens, channels), F32),
        pltpu.VMEM((STATE_SIZE, channels), F32),
        *[pltpu.VMEM(hops, BF16) for _ in range(6)],
        pltpu.VMEM((STATE_SIZE, channels), BF16),
        pltpu.VMEM((tokens, channels + query.shape[1]), BF16),
        pltpu.VMEM((n_head - 1, tokens, out_width), BF16),
        pltpu.VMEM((n_head - 1, tokens, out_width), BF16),
        dma((2,)),
        dma((2, 2)),
        dma((n_seq,)),
        dma((n_seq,)),
        dma((n_seq,)),
        dma((n_seq,)),
        *[dma((chunks,)) for _ in range(6)],
        dma((n_head - 1,)),
        dma((n_head - 1,)),
    ]
    return pl.pallas_call(
        functools.partial(kernel, n_seq, n_head),
        out_shape=jax.ShapeDtypeStruct((tokens, out_width), BF16),
        in_specs=[vmem] * 13 + [hbm] * 2,
        out_specs=vmem,
        scratch_shapes=scratch,
        compiler_params=pltpu.CompilerParams(
            collective_id=0, has_side_effects=True, vmem_limit_bytes=48 * 2**20
        ),
        name="mixer",
    )(
        inner,
        groups,
        gate,
        step,
        bias.reshape(1, -1),
        decay.reshape(1, -1),
        taps_i,
        taps_g,
        gain.reshape(1, -1),
        query,
        key,
        value,
        segs.reshape(1, -1),
        mproj,
        aproj,
    )


def solution(mesh):
    placed = (
        P("seq", "head"),
        P("seq", None),
        P("seq", "head"),
        P("head", "seq"),
        P("head"),
        P("head"),
        P(None, "head"),
        P(),
        P("head"),
        P("seq", "head"),
        P("seq", None),
        P("seq", None),
        P("seq"),
        P("head", None),
        P("head", None),
    )
    return jax.shard_map(
        functools.partial(shards, mesh.shape["seq"], mesh.shape["head"]),
        mesh=mesh,
        in_specs=placed,
        out_specs=P("seq", "head"),
        check_vma=False,
    )
```

time: 244 us -> 53.4 us (0.22); the launches traced: 240 us -> 52.8 us
  blocking collectives: 81.4 us -> 0 us
  waiting for transfers between devices: 43.1 us -> 0 us
  other arithmetic: 41.5 us -> 0 us
  Pallas kernels: 0 us -> 39 us
  matrix products: 25.2 us -> 0 us
  between operations: 15.7 us -> 0.02 us
  local copies, waits for them, and re-layouts: 21.2 us -> 13.8 us
  starting transfers between devices: 7 us -> 0 us
  loops' own time: 5.2 us -> 0 us
    all_gather x3 -> x0, blocking collectives: 65.8 us -> none  [the longest x1 26.6 us: shards(): piece_keys = lax.all_gather(my_keys, 'seq', axis=0, tiled=True)]
    pallas_call x0 -> x1, Pallas kernels: none -> 39 us  [shards(): pl.pallas_call(functools.partial(kernel, n_seq, n_head), out_shape=jax.Sh...]
    dot_general x22 -> x0, matrix products: 25.2 us -> none  [the longest x8 7.85 us: one_block(): jnp.einsum('hqk,kd->hqd', weights.astype(jnp.bfloat16), block_values, pre...]
    reduce_scatter x1 -> x0, waiting for transfers between devices: 24.1 us -> none  [shards(): lax.psum_scatter(terms.astype(jnp.bfloat16), 'head', scatter_dimension=1,...]
    all_gather x1 -> x0, waiting for transfers between devices: 19 us -> none  [entering(): lax.all_gather(part.astype(kind), axis)]
    select_n x8 -> x0, other arithmetic: 18.1 us -> none  [turn(): return jax.tree.map(lambda a, b: jnp.where(reached, a, b), new, before)]
    convert_element_type x27 -> x0, other arithmetic: 16.6 us -> none  [the longest x8 5.48 us: one_block(): key_seg = block_marks.astype(jnp.float32).astype(jnp.int32)]
    unnamed x1 -> x0, blocking collectives: 15.5 us -> none
  transfers between devices with their start and end apart: 5 -> 0, of which waited for: 2 -> 0; matrix products, arithmetic and copies ran while one was open for 24% -> 0% of each run, Pallas kernels for 0% -> 0%
where the time goes in v1:
time: 53.4 us; the launch traced here: 52.8 us
  Pallas kernels  39 us (73%)
  local copies, waits for them, and re-layouts  13.8 us (26%)
    pallas_call x1, Pallas kernels, shards(): pl.pallas_call(functools.partial(kernel, n_seq, n_head), out_shape=jax.Sh...  39 us
    unnamed x29, local copies, waits for them, and re-layouts  13.1 us

profile of v1, /device:TPU:25, one launch (start us, length us, event | category | flops | bytes accessed | tf_op | source)
XLA Modules:
  0.0 52.8 jit_solution(2776661547827902225)
XLA Ops:
  0.0 0.7 %reshape.14.gain_ref = f32[1,768]{1,0:T(1,128)S(1)} reshape(f32[768]{0:T(1024)} %param.23) | data formatting | bytes 6144 | tf_op jit(solution)/shard_map/reshape | solution.py:473
  0.7 0.0 copy-start
  0.7 1.9 %copy-done = bf16[768,2048]{1,0:T(8,128)(2,1)S(1)} copy-done((bf16[768,2048]{1,0:T(8,128)(2,1)S(1)}, bf16[768,2048]{1,0:T(8,128)(2,1)}, u32[]{:S(2)}) %copy-start) | copy-done | bytes 3145752
  2.6 0.0 copy-start.1
  2.6 1.2 %copy-done.1 = bf16[256,2048]{1,0:T(8,128)(2,1)S(1)} copy-done((bf16[256,2048]{1,0:T(8,128)(2,1)S(1)}, bf16[256,2048]{1,0:T(8,128)(2,1)}, u32[]{:S(2)}) %copy-start.1) | copy-done | bytes 1048600
  3.8 0.0 copy-start.2
  3.8 0.9 %copy-done.2 = bf16[128,768]{1,0:T(8,128)(2,1)S(1)} copy-done((bf16[128,768]{1,0:T(8,128)(2,1)S(1)}, bf16[128,768]{1,0:T(8,128)(2,1)}, u32[]{:S(2)}) %copy-start.2) | copy-done | bytes 196632
  4.7 0.0 copy-start.3
  4.7 0.9 %copy-done.3 = bf16[128,768]{1,0:T(8,128)(2,1)S(1)} copy-done((bf16[128,768]{1,0:T(8,128)(2,1)S(1)}, bf16[128,768]{1,0:T(8,128)(2,1)}, u32[]{:S(2)}) %copy-start.3) | copy-done | bytes 196632
  5.7 0.0 copy-start.4
  5.7 0.9 %copy-done.4 = bf16[128,512]{1,0:T(8,128)(2,1)S(1)} copy-done((bf16[128,512]{1,0:T(8,128)(2,1)S(1)}, bf16[128,512]{1,0:T(8,128)(2,1)}, u32[]{:S(2)}) %copy-start.4) | copy-done | bytes 131096
  6.6 0.0 copy-start.5
  6.6 0.8 %copy-done.5 = bf16[128,256]{1,0:T(8,128)(2,1)S(1)} copy-done((bf16[128,256]{1,0:T(8,128)(2,1)S(1)}, bf16[128,256]{1,0:T(8,128)(2,1)}, u32[]{:S(2)}) %copy-start.5) | copy-done | bytes 65560
  7.4 0.0 copy-start.6
  7.4 0.8 %copy-done.6 = bf16[128,256]{1,0:T(8,128)(2,1)S(1)} copy-done((bf16[128,256]{1,0:T(8,128)(2,1)S(1)}, bf16[128,256]{1,0:T(8,128)(2,1)}, u32[]{:S(2)}) %copy-start.6) | copy-done | bytes 65560
  8.2 0.8 %copy-done.7 = bf16[128,256]{1,0:T(8,128)(2,1)S(1)} copy-done((bf16[128,256]{1,0:T(8,128)(2,1)S(1)}, bf16[128,256]{1,0:T(8,128)(2,1)}, u32[]{:S(2)}) %copy-start.7) | copy-done | bytes 65560
  9.1 0.7 %copy-done.8 = f32[4,768]{1,0:T(4,128)S(1)} copy-done((f32[4,768]{1,0:T(4,128)S(1)}, f32[4,768]{1,0:T(4,128)}, u32[]{:S(2)}) %copy-start.8) | copy-done | bytes 12312
  9.8 0.7 %copy-done.9 = f32[12,128]{1,0:T(8,128)S(1)} copy-done((f32[12,128]{1,0:T(8,128)S(1)}, f32[12,128]{1,0:T(8,128)}, u32[]{:S(2)}) %copy-start.9) | copy-done | bytes 6168
  10.5 0.7 %copy-done.10 = f32[4,512]{1,0:T(4,128)S(1)} copy-done((f32[4,512]{1,0:T(4,128)S(1)}, f32[4,512]{1,0:T(4,128)}, u32[]{:S(2)}) %copy-start.10) | copy-done | bytes 8216
  11.2 0.7 %copy-done.11 = f32[12]{0:T(128)S(1)} copy-done((f32[12]{0:T(128)S(1)}, f32[12]{0:T(128)}, u32[]{:S(2)}) %copy-start.11) | copy-done | bytes 72
  11.8 0.7 %copy-done.12 = f32[12]{0:T(128)S(1)} copy-done((f32[12]{0:T(128)S(1)}, f32[12]{0:T(128)}, u32[]{:S(2)}) %copy-start.12) | copy-done | bytes 72
  12.5 0.7 %copy-done.13 = s32[128]{0:T(128)S(1)} copy-done((s32[128]{0:T(128)S(1)}, s32[128]{0:T(128)}, u32[]{:S(2)}) %copy-start.13) | copy-done | bytes 536
  13.2 39.0 %mixer.1 = bf16[128,512]{1,0:T(8,128)(2,1)S(1)} custom-call(bf16[128,768]{1,0:T(8,128)(2,1)S(1)} %copy-done.2, bf16[128,512]{1,0:T(8,128)(2,1)S(1)} %copy-done.4, bf16[128,768]{1,0:T(8,128)(2,1)S(1)} %copy-done.3, f32[12,128]{1,0:T(8,128)S(1)} %copy-done.9, f32[1,12]{1,0:T(1,128)S(1)} %bitcast.3, f32[1,12]{1,0:T(1,128)S(1)} %bitcast.4, ...), custom_call_target="tpu_custom_call" | custom-call | tf_op jit(solution)/shard_map/mixer/pallas_call | solution.py:454
  52.2 0.7 %copy.17 = bf16[128,512]{1,0:T(8,128)(2,1)} copy(bf16[128,512]{1,0:T(8,128)(2,1)S(1)} %mixer.1) | data formatting | bytes 262144
  (7 shorter events, 0.0 us)
Async XLA Ops:
  0.7 1.9 %copy-start = (bf16[768,2048]{1,0:T(8,128)(2,1)S(1)}, bf16[768,2048]{1,0:T(8,128)(2,1)}, u32[]{:S(2)}) copy-start(bf16[768,2048]{1,0:T(8,128)(2,1)} %mamba_proj_hbm.1) | copy-start | bytes 9437188
  2.6 1.2 %copy-start.1 = (bf16[256,2048]{1,0:T(8,128)(2,1)S(1)}, bf16[256,2048]{1,0:T(8,128)(2,1)}, u32[]{:S(2)}) copy-start(bf16[256,2048]{1,0:T(8,128)(2,1)} %attn_proj_hbm.1) | copy-start | bytes 3145732
  3.8 0.9 %copy-start.2 = (bf16[128,768]{1,0:T(8,128)(2,1)S(1)}, bf16[128,768]{1,0:T(8,128)(2,1)}, u32[]{:S(2)}) copy-start(bf16[128,768]{1,0:T(8,128)(2,1)} %inner_ref.1) | copy-start | bytes 589828
  4.7 0.9 %copy-start.3 = (bf16[128,768]{1,0:T(8,128)(2,1)S(1)}, bf16[128,768]{1,0:T(8,128)(2,1)}, u32[]{:S(2)}) copy-start(bf16[128,768]{1,0:T(8,128)(2,1)} %gate_ref.1) | copy-start | bytes 589828
  5.7 0.9 %copy-start.4 = (bf16[128,512]{1,0:T(8,128)(2,1)S(1)}, bf16[128,512]{1,0:T(8,128)(2,1)}, u32[]{:S(2)}) copy-start(bf16[128,512]{1,0:T(8,128)(2,1)} %groups_ref.1) | copy-start | bytes 393220
  6.6 0.8 %copy-start.5 = (bf16[128,256]{1,0:T(8,128)(2,1)S(1)}, bf16[128,256]{1,0:T(8,128)(2,1)}, u32[]{:S(2)}) copy-start(bf16[128,256]{1,0:T(8,128)(2,1)} %query_ref.1) | copy-start | bytes 196612
  7.4 0.8 %copy-start.6 = (bf16[128,256]{1,0:T(8,128)(2,1)S(1)}, bf16[128,256]{1,0:T(8,128)(2,1)}, u32[]{:S(2)}) copy-start(bf16[128,256]{1,0:T(8,128)(2,1)} %key_ref.1) | copy-start | bytes 196612
  8.2 0.8 %copy-start.7 = (bf16[128,256]{1,0:T(8,128)(2,1)S(1)}, bf16[128,256]{1,0:T(8,128)(2,1)}, u32[]{:S(2)}) copy-start(bf16[128,256]{1,0:T(8,128)(2,1)} %value_ref.1) | copy-start | bytes 196612
  9.1 0.7 %copy-start.8 = (f32[4,768]{1,0:T(4,128)S(1)}, f32[4,768]{1,0:T(4,128)}, u32[]{:S(2)}) copy-start(f32[4,768]{1,0:T(4,128)} %taps_inner_ref.1) | copy-start | bytes 36868
  9.8 0.7 %copy-start.9 = (f32[12,128]{1,0:T(8,128)S(1)}, f32[12,128]{1,0:T(8,128)}, u32[]{:S(2)}) copy-start(f32[12,128]{1,0:T(8,128)} %step_ref.1) | copy-start | bytes 18436
  10.5 0.7 %copy-start.10 = (f32[4,512]{1,0:T(4,128)S(1)}, f32[4,512]{1,0:T(4,128)}, u32[]{:S(2)}) copy-start(f32[4,512]{1,0:T(4,128)} %taps_groups_ref.1) | copy-start | bytes 24580
  11.2 0.7 %copy-start.11 = (f32[12]{0:T(128)S(1)}, f32[12]{0:T(128)}, u32[]{:S(2)}) copy-start(f32[12]{0:T(128)} %param.19) | copy-start | bytes 148
  11.8 0.7 %copy-start.12 = (f32[12]{0:T(128)S(1)}, f32[12]{0:T(128)}, u32[]{:S(2)}) copy-start(f32[12]{0:T(128)} %param.20) | copy-start | bytes 148
  12.5 0.7 %copy-start.13 = (s32[128]{0:T(128)S(1)}, s32[128]{0:T(128)}, u32[]{:S(2)}) copy-start(s32[128]{0:T(128)} %param.27) | copy-start | bytes 1540

commit v2 on v1

--- a/solution.py
+++ b/solution.py
@@ -40,6 +40,22 @@
 def kernel(
     n_seq,
     n_head,
+    inner_hbm,
+    groups_hbm,
+    gate_hbm,
+    step_hbm,
+    bias_hbm,
+    decay_hbm,
+    taps_inner_hbm,
+    taps_groups_hbm,
+    gain_hbm,
+    query_hbm,
+    key_hbm,
+    value_hbm,
+    segs_hbm,
+    mamba_proj_hbm,
+    attn_proj_hbm,
+    out_ref,
     inner_ref,
     groups_ref,
     gate_ref,
@@ -53,9 +69,6 @@
     key_ref,
     value_ref,
     segs_ref,
-    mamba_proj_hbm,
-    attn_proj_hbm,
-    out_ref,
     mproj,
     aproj,
     pad_inner,
@@ -75,16 +88,23 @@
     e_recv,
     f_send,
     f_recv,
-    entering,
+    partner_c,
+    carried_ref,
+    through,
     both,
     rs_send,
     rs_recv,
+    load_sem,
     weight_sem,
     rim_sem,
     meta_ss,
     meta_rs,
     kv_ss,
     kv_rs,
+    share_ss,
+    share_rs,
+    c_ss,
+    c_rs,
     s_ss,
     s_rs,
     e_ss,
@@ -104,6 +124,10 @@
     pair, side = me // 2, me % 2
     last_pair = n_seq // 2 - 1
     heads_here = query_ref.shape[1] // HD
+    core = mine % 2
+    sibling = mine + 1 - 2 * core
+    opposite = (mine + 2) % n_head
+    opposite_sibling = (sibling + 2) % n_head
 
     def at_seq(s):
         return (s, mine)
@@ -115,7 +139,27 @@
         pltpu.make_async_copy(mamba_proj_hbm, mproj, weight_sem.at[0]),
         pltpu.make_async_copy(attn_proj_hbm, aproj, weight_sem.at[1]),
     ]
-    for w in weights:
+    loads = [
+        pltpu.make_async_copy(src, dst, load_sem.at[i])
+        for i, (src, dst) in enumerate(
+            (
+                (step_hbm, step_ref),
+                (bias_hbm, bias_ref),
+                (decay_hbm, decay_ref),
+                (segs_hbm, segs_ref),
+                (key_hbm, key_ref),
+                (value_hbm, value_ref),
+                (inner_hbm, inner_ref),
+                (groups_hbm, groups_ref),
+                (taps_inner_hbm, taps_inner_ref),
+                (taps_groups_hbm, taps_groups_ref),
+                (query_hbm, query_ref),
+                (gate_hbm, gate_ref),
+                (gain_hbm, gain_ref),
+            )
+        )
+    ]
+    for w in loads + weights:
         w.start()
 
     barrier = pltpu.get_barrier_semaphore()
@@ -124,14 +168,16 @@
     for d in range(1, n_head):
         pl.semaphore_signal(barrier, inc=1, device_id=at_head((mine + d) % n_head), device_id_type=MESH)
 
+    for w in loads[:6]:
+        w.wait()
     kv_head = mine * heads_here // (QH // KVH)
     kv_cols = pl.ds(pl.multiple_of(kv_head * HD, HD), HD)
-    kv[me, :, 0:HD] = key_ref[:, kv_cols]
-    kv[me, :, HD : 2 * HD] = value_ref[:, kv_cols]
-
-    raw = step_ref[...] + column(bias_ref[...])
+    kv[me, 0] = key_ref[:, kv_cols]
+    kv[me, 1] = value_ref[:, kv_cols]
+
+    raw = step_ref[...] + column(bias_ref[...].reshape(1, heads))
     steps = jnp.maximum(raw, 0.0) + jnp.log1p(jnp.exp(-jnp.abs(raw)))
-    rates = jnp.exp(column(decay_ref[...]))
+    rates = jnp.exp(column(decay_ref[...].reshape(1, heads)))
     row_t, col_t = iota((tokens, tokens), 0), iota((tokens, tokens), 1)
     upto = (row_t <= col_t).astype(F32)
     cumul = dot(-steps * rates, upto, (1, 0), HIGHEST)
@@ -139,12 +185,17 @@
     cumx[...] = dot(cumul, spread, (0, 0), HIGHEST)
     stepx = dot(steps, spread, (0, 0), HIGHEST)
     total_row = cumx[tokens - 1 : tokens, :]
-    segs_row = segs_ref[...].astype(F32)
+    segs_row = segs_ref[...].reshape(1, tokens).astype(F32)
     segs_col = column(segs_row)
     last_seg = segs_row[:, tokens - 1 : tokens]
-    meta[me, 0:1, :] = total_row
-    meta[me, 1:2, 0:tokens] = segs_row
-    meta[me, 2:3, :] = jnp.broadcast_to(last_seg, (1, channels))
+    eye = (iota((heads, heads), 0) == iota((heads, heads), 1)).astype(F32)
+    cum_cols = dot(cumul, eye, (0, 0), HIGHEST)
+    meta[me] = jnp.zeros(meta.shape[1:], F32)
+    meta[me, 0:1, 0:heads] = cum_cols[tokens - 1 : tokens, :]
+    meta[me, 1:2, :] = segs_row
+    meta[me, 2:3, :] = jnp.broadcast_to(last_seg, (1, tokens))
+    for w in loads[6:]:
+        w.wait()
     pl.semaphore_wait(barrier, n_seq + n_head - 2)
 
     def rim_copies(target):
@@ -163,7 +214,22 @@
 
     def kv_copy(slot, other):
         return pltpu.make_async_remote_copy(
-            kv.at[slot], kv.at[slot], kv_ss.at[other], kv_rs.at[slot], device_id=at_seq(other), device_id_type=MESH
+            kv.at[slot, core],
+            kv.at[slot, core],
+            kv_ss.at[other],
+            kv_rs.at[slot],
+            device_id=at_seq(other),
+            device_id_type=MESH,
+        )
+
+    def kv_share(slot):
+        return pltpu.make_async_remote_copy(
+            kv.at[slot, core],
+            kv.at[slot, core],
+            share_ss.at[slot],
+            share_rs.at[slot],
+            device_id=at_head(sibling),
+            device_id_type=MESH,
         )
 
     following = lax.min(me + 1, n_seq - 1)
@@ -211,7 +277,7 @@
 
     taps = taps_inner_ref.shape[0]
     prev_last = meta[previous, 2:3, 0:1]
-    prev_segs = meta[previous, 1:2, 0:tokens]
+    prev_segs = meta[previous, 1:2, :]
     token_col = iota((tokens, 1), 0)
     keeps = []
     for k in range(taps - 1):
@@ -262,10 +328,20 @@
         s_send[c] = state[:, part(1 - side, c)].astype(BF16)
         hop(s_send, s_recv, s_ss, s_rs, c, partner).start()
 
+    def c_copy():
+        return pltpu.make_async_remote_copy(
+            conv_bc.at[:, pl.ds(STATE_SIZE, STATE_SIZE)],
+            partner_c,
+            c_ss.at[0],
+            c_rs.at[0],
+            device_id=at_seq(partner),
+            device_id_type=MESH,
+        )
+
+    c_copy().start()
+
     crossing = dot(read_c, read_b, (1, 1))
     live = (jnp.broadcast_to(segs_row, (tokens, tokens)) == segs_col) & (row_t >= col_t)
-    eye = (iota((heads, heads), 0) == iota((heads, heads), 1)).astype(F32)
-    cum_cols = dot(cumul, eye, (0, 0), HIGHEST)
     left = iota((tokens, LANES), 1) < HEAD_CHANNELS
     for p in range(pairs):
         got = []
@@ -281,16 +357,23 @@
     segs_rows = jnp.concatenate([segs_col] * heads_here, axis=0)
     token_rows = jnp.concatenate([token_col] * heads_here, axis=0)
 
+    def share(d, _):
+        kv_copy(me - d, me).wait_recv()
+        kv_share(me - d).start()
+        return 0
+
+    lax.fori_loop(1, me + 1, share, 0)
+
     def attend(d, carry):
         top, total, summed = carry
         k = me - d
 
         @pl.when(d > 0)
         def _():
-            kv_copy(k, k).wait_recv()
-
-        scores = dot(queries, kv[k, :, 0:HD], (1, 1)) * scale
-        allowed = (meta[k, 1:2, 0:tokens] == segs_rows) & (
+            kv_share(k).wait_recv()
+
+        scores = dot(queries, kv[k, 0], (1, 1)) * scale
+        allowed = (meta[k, 1:2, :] == segs_rows) & (
             iota((rows, tokens), 1) + (k - me) * tokens <= token_rows
         )
         scores = jnp.where(allowed, scores, -jnp.inf)
@@ -298,7 +381,7 @@
         rescale = jnp.exp(top - new_top)
         w = jnp.exp(scores - new_top)
         total = total * rescale + jnp.sum(w, axis=1, keepdims=True)
-        summed = summed * rescale + dot(w.astype(BF16), kv[k, :, HD : 2 * HD], (1, 0))
+        summed = summed * rescale + dot(w.astype(BF16), kv[k, 1], (1, 0))
         return new_top, total, summed
 
     top, total, summed = lax.fori_loop(
@@ -316,14 +399,21 @@
         e_recv[...] = jnp.zeros_like(e_recv)
 
     first, second = pair * 2, pair * 2 + 1
-    seg_before = meta[lax.max(first - 1, 0), 2:3, 0:LANES]
-    seg_first = meta[first, 2:3, 0:LANES]
-    seg_second = meta[second, 2:3, 0:LANES]
+    seg_before = meta[lax.max(first - 1, 0), 2:3, 0:1]
+    seg_first = meta[first, 2:3, 0:1]
+    seg_second = meta[second, 2:3, 0:1]
+    through[0:1, :] = jnp.where(
+        seg_first == seg_before, jnp.exp(dot(meta[first, 0:1, 0:heads], spread, (1, 0), HIGHEST)), 0.0
+    )
+    through[1:2, :] = jnp.where(
+        seg_second == seg_first, jnp.exp(dot(meta[second, 0:1, 0:heads], spread, (1, 0), HIGHEST)), 0.0
+    )
+    c_copy().wait_recv()
     on_left = side == 0
     for c in range(chunks):
         cols = part(side, c)
-        through_first = jnp.where(seg_first == seg_before, jnp.exp(meta[first, 0:1, cols]), 0.0)
-        through_second = jnp.where(seg_second == seg_first, jnp.exp(meta[second, 0:1, cols]), 0.0)
+        through_first = through[0:1, cols]
+        through_second = through[1:2, cols]
         hop(s_send, s_recv, s_ss, s_rs, c, partner).wait_recv()
         own, others = state[:, cols], s_recv[c].astype(F32)
 
@@ -339,23 +429,26 @@
             e_send[c] = (through_second * enter_second + jnp.where(on_left, others, own)).astype(BF16)
             hop(e_send, e_recv, e_ss, e_rs, c, upper).start()
 
-        f_send[c] = jnp.where(on_left, enter_second, enter_first).astype(BF16)
+        theirs = jnp.where(on_left, enter_second, enter_first).astype(BF16)
+        f_send[c] = dot(partner_c[...], theirs, (1, 0)).astype(BF16)
         hop(f_send, f_recv, f_ss, f_rs, c, partner).start()
-        entering[:, cols] = jnp.where(on_left, enter_first, enter_second).astype(BF16)
+        ours = jnp.where(on_left, enter_first, enter_second).astype(BF16)
+        carried_ref[:, cols] = dot(read_c, ours, (1, 0))
 
     for c in range(chunks):
         hop(f_send, f_recv, f_ss, f_rs, c, partner).wait_recv()
-        entering[:, part(1 - side, c)] = f_recv[c]
+        carried_ref[:, part(1 - side, c)] = f_recv[c].astype(F32)
 
     joined = segs_col == prev_last
+    gain_row = gain_ref[...].reshape(1, channels)
     same_head = (iota((LANES, LANES), 0) // HEAD_CHANNELS == iota((LANES, LANES), 1) // HEAD_CHANNELS).astype(F32)
     for p in range(pairs):
         cols = slice(p * LANES, (p + 1) * LANES)
-        carried = dot(read_c, entering[:, cols], (1, 0))
+        carried = carried_ref[:, cols]
         y = y_ref[:, cols] + jnp.where(joined, jnp.exp(cumx[:, cols]), 0.0) * carried
         gated = y * jax.nn.silu(gate_ref[:, cols].astype(F32))
         mean_square = dot(gated * gated, same_head, (1, 0), HIGHEST) * (1.0 / HEAD_CHANNELS)
-        both[:, cols] = (gated * lax.rsqrt(mean_square + 1e-05) * gain_ref[:, cols]).astype(BF16)
+        both[:, cols] = (gated * lax.rsqrt(mean_square + 1e-05) * gain_row[:, cols]).astype(BF16)
 
     for w in weights:
         w.wait()
@@ -365,28 +458,34 @@
         cols = pl.ds(pl.multiple_of(j * width, LANES), width)
         return dot(both[:, :channels], mproj[:, cols], (1, 0)) + dot(both[:, channels:], aproj[:, cols], (1, 0))
 
-    def rs_copy(d):
+    def rs_copy(i, target):
         return pltpu.make_async_remote_copy(
-            rs_send.at[d - 1],
-            rs_recv.at[d - 1],
-            rs_ss.at[d - 1],
-            rs_rs.at[d - 1],
-            device_id=at_head((mine + d) % n_head),
-            device_id_type=MESH,
-        )
-
-    turns = sorted(range(1, n_head), key=lambda d: abs(d - n_head // 2))
-    for d in turns:
-        rs_send[d - 1] = product((mine + d) % n_head).astype(BF16)
-        rs_copy(d).start()
+            rs_send.at[i], rs_recv.at[i], rs_ss.at[i], rs_rs.at[i], device_id=at_head(target), device_id_type=MESH
+        )
+
+    to_pair, to_sibling, to_opposite = rs_copy(0, sibling), rs_copy(1, sibling), rs_copy(2, opposite)
+    rs_send[0] = product(opposite_sibling).astype(BF16)
+    to_pair.start()
+    rs_send[1] = product(sibling).astype(BF16)
+    to_sibling.start()
+    away = product(opposite)
+    to_pair.wait_recv()
+    rs_send[2] = (away + rs_recv[0].astype(F32)).astype(BF16)
+    to_opposite.start()
     result = product(mine)
-    for d in turns:
-        rs_copy(d).wait_recv()
-        result = result + rs_recv[d - 1].astype(F32)
-    out_ref[...] = result.astype(BF16)
-
-    for d in turns:
-        rs_copy(d).wait_send()
+    to_sibling.wait_recv()
+    result = result + rs_recv[1].astype(F32)
+    to_opposite.wait_recv()
+    out_ref[...] = (result + rs_recv[2].astype(F32)).astype(BF16)
+
+    for copy in (to_pair, to_sibling, to_opposite, c_copy()):
+        copy.wait_send()
+
+    def sent_share(d, _):
+        kv_share(me - d).wait_send()
+        return 0
+
+    lax.fori_loop(1, me + 1, sent_share, 0)
 
     @pl.when(me < n_seq - 1)
     def _():
@@ -420,33 +519,42 @@
     chunks = channels // 2 // LANES
     hops = (chunks, STATE_SIZE, LANES)
     vmem = pl.BlockSpec(memory_space=pltpu.VMEM)
-    hbm = pl.BlockSpec(memory_space=pl.ANY)
+    hbm = pl.BlockSpec(memory_space=pltpu.HBM)
     dma = pltpu.SemaphoreType.DMA
     scratch = [
+        *[pltpu.VMEM(a.shape, a.dtype) for a in arrays[:13]],
         pltpu.VMEM(mproj.shape, BF16),
         pltpu.VMEM(aproj.shape, BF16),
         pltpu.VMEM((tokens + RIM, channels), F32),
         pltpu.VMEM((tokens + RIM, groups.shape[1]), F32),
         pltpu.VMEM((RIM, channels), BF16),
         pltpu.VMEM((RIM, groups.shape[1]), BF16),
-        pltpu.VMEM((n_seq, 8, channels), F32),
-        pltpu.VMEM((n_seq, tokens, 2 * HD), BF16),
+        pltpu.VMEM((n_seq, 8, tokens), F32),
+        pltpu.VMEM((n_seq, 2, tokens, HD), BF16),
         pltpu.VMEM((tokens, channels), BF16),
         pltpu.VMEM((tokens, groups.shape[1]), BF16),
         pltpu.VMEM((tokens, channels), F32),
         pltpu.VMEM((tokens, channels), F32),
         pltpu.VMEM((STATE_SIZE, channels), F32),
-        *[pltpu.VMEM(hops, BF16) for _ in range(6)],
-        pltpu.VMEM((STATE_SIZE, channels), BF16),
+        *[pltpu.VMEM(hops, BF16) for _ in range(4)],
+        *[pltpu.VMEM((chunks, tokens, LANES), BF16) for _ in range(2)],
+        pltpu.VMEM((tokens, STATE_SIZE), BF16),
+        pltpu.VMEM((tokens, channels), F32),
+        pltpu.VMEM((8, channels), F32),
         pltpu.VMEM((tokens, channels + query.shape[1]), BF16),
         pltpu.VMEM((n_head - 1, tokens, out_width), BF16),
         pltpu.VMEM((n_head - 1, tokens, out_width), BF16),
+        dma((13,)),
         dma((2,)),
         dma((2, 2)),
         dma((n_seq,)),
         dma((n_seq,)),
         dma((n_seq,)),
         dma((n_seq,)),
+        dma((n_seq,)),
+        dma((n_seq,)),
+        dma((1,)),
+        dma((1,)),
         *[dma((chunks,)) for _ in range(6)],
         dma((n_head - 1,)),
         dma((n_head - 1,)),
@@ -454,7 +562,7 @@
     return pl.pallas_call(
         functools.partial(kernel, n_seq, n_head),
         out_shape=jax.ShapeDtypeStruct((tokens, out_width), BF16),
-        in_specs=[vmem] * 13 + [hbm] * 2,
+        in_specs=[hbm] * 15,
         out_specs=vmem,
         scratch_shapes=scratch,
         compiler_params=pltpu.CompilerParams(
@@ -466,15 +574,15 @@
         groups,
         gate,
         step,
-        bias.reshape(1, -1),
-        decay.reshape(1, -1),
+        bias,
+        decay,
         taps_i,
         taps_g,
-        gain.reshape(1, -1),
+        gain,
         query,
         key,
         value,
-        segs.reshape(1, -1),
+        segs,
         mproj,
         aproj,
     )

time: 53.4 us -> 52 us (0.974)
  Pallas kernels: 39 us -> 37.6 us
    pallas_call x1, Pallas kernels: 39 us -> 37.6 us  [shards(): pl.pallas_call(functools.partial(kernel, n_seq, n_head), out_shape=jax.Sh...]
    reshape x1 -> x0, local copies, waits for them, and re-layouts: 0.69 us -> none  [shards(): gain.reshape(1, -1)]
    unnamed x29 -> x31, local copies, waits for them, and re-layouts: 13.1 us -> 13.8 us
where the time goes in v2:
time: 52 us; the launch traced here: 51.4 us
  Pallas kernels  37.6 us (72%)
  local copies, waits for them, and re-layouts  13.8 us (27%)
    pallas_call x1, Pallas kernels, shards(): pl.pallas_call(functools.partial(kernel, n_seq, n_head), out_shape=jax.Sh...  37.6 us
    unnamed x31, local copies, waits for them, and re-layouts  13.8 us

profile of v2, /device:TPU:25, one launch (start us, length us, event | category | flops | bytes accessed | tf_op | source)
XLA Modules:
  0.0 51.4 jit_solution(8736940348240004280)
XLA Ops:
  0.0 0.0 copy-start
  0.0 1.9 %copy-done = bf16[768,2048]{1,0:T(8,128)(2,1)S(1)} copy-done((bf16[768,2048]{1,0:T(8,128)(2,1)S(1)}, bf16[768,2048]{1,0:T(8,128)(2,1)}, u32[]{:S(2)}) %copy-start) | copy-done | bytes 3145752
  1.9 0.0 copy-start.1
  1.9 1.2 %copy-done.1 = bf16[256,2048]{1,0:T(8,128)(2,1)S(1)} copy-done((bf16[256,2048]{1,0:T(8,128)(2,1)S(1)}, bf16[256,2048]{1,0:T(8,128)(2,1)}, u32[]{:S(2)}) %copy-start.1) | copy-done | bytes 1048600
  3.1 0.0 copy-start.2
  3.1 0.9 %copy-done.2 = bf16[128,768]{1,0:T(8,128)(2,1)S(1)} copy-done((bf16[128,768]{1,0:T(8,128)(2,1)S(1)}, bf16[128,768]{1,0:T(8,128)(2,1)}, u32[]{:S(2)}) %copy-start.2) | copy-done | bytes 196632
  4.0 0.0 copy-start.3
  4.0 0.9 %copy-done.3 = bf16[128,768]{1,0:T(8,128)(2,1)S(1)} copy-done((bf16[128,768]{1,0:T(8,128)(2,1)S(1)}, bf16[128,768]{1,0:T(8,128)(2,1)}, u32[]{:S(2)}) %copy-start.3) | copy-done | bytes 196632
  5.0 0.0 copy-start.4
  5.0 0.9 %copy-done.4 = bf16[128,512]{1,0:T(8,128)(2,1)S(1)} copy-done((bf16[128,512]{1,0:T(8,128)(2,1)S(1)}, bf16[128,512]{1,0:T(8,128)(2,1)}, u32[]{:S(2)}) %copy-start.4) | copy-done | bytes 131096
  5.9 0.0 copy-start.5
  5.9 0.8 %copy-done.5 = bf16[128,256]{1,0:T(8,128)(2,1)S(1)} copy-done((bf16[128,256]{1,0:T(8,128)(2,1)S(1)}, bf16[128,256]{1,0:T(8,128)(2,1)}, u32[]{:S(2)}) %copy-start.5) | copy-done | bytes 65560
  6.7 0.0 copy-start.6
  6.7 0.8 %copy-done.6 = bf16[128,256]{1,0:T(8,128)(2,1)S(1)} copy-done((bf16[128,256]{1,0:T(8,128)(2,1)S(1)}, bf16[128,256]{1,0:T(8,128)(2,1)}, u32[]{:S(2)}) %copy-start.6) | copy-done | bytes 65560
  7.6 0.8 %copy-done.7 = bf16[128,256]{1,0:T(8,128)(2,1)S(1)} copy-done((bf16[128,256]{1,0:T(8,128)(2,1)S(1)}, bf16[128,256]{1,0:T(8,128)(2,1)}, u32[]{:S(2)}) %copy-start.7) | copy-done | bytes 65560
  8.4 0.7 %copy-done.8 = f32[4,768]{1,0:T(4,128)S(1)} copy-done((f32[4,768]{1,0:T(4,128)S(1)}, f32[4,768]{1,0:T(4,128)}, u32[]{:S(2)}) %copy-start.8) | copy-done | bytes 12312
  9.1 0.7 %copy-done.9 = f32[12,128]{1,0:T(8,128)S(1)} copy-done((f32[12,128]{1,0:T(8,128)S(1)}, f32[12,128]{1,0:T(8,128)}, u32[]{:S(2)}) %copy-start.9) | copy-done | bytes 6168
  9.8 0.7 %copy-done.10 = f32[4,512]{1,0:T(4,128)S(1)} copy-done((f32[4,512]{1,0:T(4,128)S(1)}, f32[4,512]{1,0:T(4,128)}, u32[]{:S(2)}) %copy-start.10) | copy-done | bytes 8216
  10.5 0.7 %copy-done.11 = f32[768]{0:T(1024)S(1)} copy-done((f32[768]{0:T(1024)S(1)}, f32[768]{0:T(1024)}, u32[]{:S(2)}) %copy-start.11) | copy-done | bytes 3096
  11.2 0.7 %copy-done.12 = f32[12]{0:T(128)S(1)} copy-done((f32[12]{0:T(128)S(1)}, f32[12]{0:T(128)}, u32[]{:S(2)}) %copy-start.12) | copy-done | bytes 72
  11.8 0.7 %copy-done.13 = f32[12]{0:T(128)S(1)} copy-done((f32[12]{0:T(128)S(1)}, f32[12]{0:T(128)}, u32[]{:S(2)}) %copy-start.13) | copy-done | bytes 72
  12.5 0.7 %copy-done.14 = s32[128]{0:T(128)S(1)} copy-done((s32[128]{0:T(128)S(1)}, s32[128]{0:T(128)}, u32[]{:S(2)}) %copy-start.14) | copy-done | bytes 536
  13.2 37.6 %mixer.1 = bf16[128,512]{1,0:T(8,128)(2,1)S(1)} custom-call(bf16[128,768]{1,0:T(8,128)(2,1)S(1)} %copy-done.2, bf16[128,512]{1,0:T(8,128)(2,1)S(1)} %copy-done.4, bf16[128,768]{1,0:T(8,128)(2,1)S(1)} %copy-done.3, f32[12,128]{1,0:T(8,128)S(1)} %copy-done.9, f32[12]{0:T(128)S(1)} %copy-done.12, f32[12]{0:T(128)S(1)} %copy-done.13, f32[4,768]{1,0:T(4,128)S(1)} %copy-done.8, ...), custom_call_target="tpu_custom_call" | custom-call | tf_op jit(solution)/shard_map/mixer/pallas_call | solution.py:562
  50.8 0.7 %copy.17 = bf16[128,512]{1,0:T(8,128)(2,1)} copy(bf16[128,512]{1,0:T(8,128)(2,1)S(1)} %mixer.1) | data formatting | bytes 262144
  (8 shorter events, 0.0 us)
Async XLA Ops:
  0.0 1.9 %copy-start = (bf16[768,2048]{1,0:T(8,128)(2,1)S(1)}, bf16[768,2048]{1,0:T(8,128)(2,1)}, u32[]{:S(2)}) copy-start(bf16[768,2048]{1,0:T(8,128)(2,1)} %mamba_proj_hbm.1) | copy-start | bytes 9437188
  1.9 1.2 %copy-start.1 = (bf16[256,2048]{1,0:T(8,128)(2,1)S(1)}, bf16[256,2048]{1,0:T(8,128)(2,1)}, u32[]{:S(2)}) copy-start(bf16[256,2048]{1,0:T(8,128)(2,1)} %attn_proj_hbm.1) | copy-start | bytes 3145732
  3.1 0.9 %copy-start.2 = (bf16[128,768]{1,0:T(8,128)(2,1)S(1)}, bf16[128,768]{1,0:T(8,128)(2,1)}, u32[]{:S(2)}) copy-start(bf16[128,768]{1,0:T(8,128)(2,1)} %inner_hbm.1) | copy-start | bytes 589828
  4.0 0.9 %copy-start.3 = (bf16[128,768]{1,0:T(8,128)(2,1)S(1)}, bf16[128,768]{1,0:T(8,128)(2,1)}, u32[]{:S(2)}) copy-start(bf16[128,768]{1,0:T(8,128)(2,1)} %gate_hbm.1) | copy-start | bytes 589828
  5.0 0.9 %copy-start.4 = (bf16[128,512]{1,0:T(8,128)(2,1)S(1)}, bf16[128,512]{1,0:T(8,128)(2,1)}, u32[]{:S(2)}) copy-start(bf16[128,512]{1,0:T(8,128)(2,1)} %groups_hbm.1) | copy-start | bytes 393220
  5.9 0.8 %copy-start.5 = (bf16[128,256]{1,0:T(8,128)(2,1)S(1)}, bf16[128,256]{1,0:T(8,128)(2,1)}, u32[]{:S(2)}) copy-start(bf16[128,256]{1,0:T(8,128)(2,1)} %query_hbm.1) | copy-start | bytes 196612
  6.7 0.8 %copy-start.6 = (bf16[128,256]{1,0:T(8,128)(2,1)S(1)}, bf16[128,256]{1,0:T(8,128)(2,1)}, u32[]{:S(2)}) copy-start(bf16[128,256]{1,0:T(8,128)(2,1)} %key_hbm.1) | copy-start | bytes 196612
  7.6 0.8 %copy-start.7 = (bf16[128,256]{1,0:T(8,128)(2,1)S(1)}, bf16[128,256]{1,0:T(8,128)(2,1)}, u32[]{:S(2)}) copy-start(bf16[128,256]{1,0:T(8,128)(2,1)} %value_hbm.1) | copy-start | bytes 196612
  8.4 0.7 %copy-start.8 = (f32[4,768]{1,0:T(4,128)S(1)}, f32[4,768]{1,0:T(4,128)}, u32[]{:S(2)}) copy-start(f32[4,768]{1,0:T(4,128)} %taps_inner_hbm.1) | copy-start | bytes 36868
  9.1 0.7 %copy-start.9 = (f32[12,128]{1,0:T(8,128)S(1)}, f32[12,128]{1,0:T(8,128)}, u32[]{:S(2)}) copy-start(f32[12,128]{1,0:T(8,128)} %step_hbm.1) | copy-start | bytes 18436
  9.8 0.7 %copy-start.10 = (f32[4,512]{1,0:T(4,128)S(1)}, f32[4,512]{1,0:T(4,128)}, u32[]{:S(2)}) copy-start(f32[4,512]{1,0:T(4,128)} %taps_groups_hbm.1) | copy-start | bytes 24580
  10.5 0.7 %copy-start.11 = (f32[768]{0:T(1024)S(1)}, f32[768]{0:T(1024)}, u32[]{:S(2)}) copy-start(f32[768]{0:T(1024)} %gain_hbm.1) | copy-start | bytes 9220
  11.2 0.7 %copy-start.12 = (f32[12]{0:T(128)S(1)}, f32[12]{0:T(128)}, u32[]{:S(2)}) copy-start(f32[12]{0:T(128)} %bias_hbm.1) | copy-start | bytes 148
  11.8 0.7 %copy-start.13 = (f32[12]{0:T(128)S(1)}, f32[12]{0:T(128)}, u32[]{:S(2)}) copy-start(f32[12]{0:T(128)} %decay_hbm.1) | copy-start | bytes 148
  12.5 0.7 %copy-start.14 = (s32[128]{0:T(128)S(1)}, s32[128]{0:T(128)}, u32[]{:S(2)}) copy-start(s32[128]{0:T(128)} %segs_hbm.1) | copy-start | bytes 1540

commit v3 on v2

--- a/solution.py
+++ b/solution.py
@@ -89,7 +89,7 @@
     f_send,
     f_recv,
     partner_c,
-    carried_ref,
+    entering,
     through,
     both,
     rs_send,
@@ -255,15 +255,9 @@
     pad_inner[RIM:, :] = inner_ref[...].astype(F32)
     pad_groups[RIM:, :] = groups_ref[...].astype(F32)
 
-    def wait_meta(d, _):
-        k = (me + d) % n_seq
-        meta_copy(k, k).wait_recv()
-        return 0
-
-    lax.fori_loop(1, n_seq, wait_meta, 0)
-
     @pl.when(me > 0)
     def _():
+        meta_copy(previous, previous).wait_recv()
         for c in rim_copies(previous):
             c.wait_recv()
 
@@ -339,6 +333,17 @@
         )
 
     c_copy().start()
+
+    def wait_meta(d, _):
+        k = (me + d) % n_seq
+        meta_copy(k, k).wait_recv()
+        return 0
+
+    lax.fori_loop(1, n_seq - 1, wait_meta, 0)
+
+    @pl.when(me == 0)
+    def _():
+        meta_copy(n_seq - 1, n_seq - 1).wait_recv()
 
     crossing = dot(read_c, read_b, (1, 1))
     live = (jnp.broadcast_to(segs_row, (tokens, tokens)) == segs_col) & (row_t >= col_t)
@@ -362,8 +367,6 @@
         kv_share(me - d).start()
         return 0
 
-    lax.fori_loop(1, me + 1, share, 0)
-
     def attend(d, carry):
         top, total, summed = carry
         k = me - d
@@ -384,15 +387,19 @@
         summed = summed * rescale + dot(w.astype(BF16), kv[k, 1], (1, 0))
         return new_top, total, summed
 
-    top, total, summed = lax.fori_loop(
-        0,
-        me + 1,
-        attend,
-        (jnp.full((rows, 1), -1e30, F32), jnp.zeros((rows, 1), F32), jnp.zeros((rows, HD), F32)),
-    )
-    attended = (summed / total).astype(BF16)
-    for h in range(heads_here):
-        both[:, channels + h * HD : channels + (h + 1) * HD] = attended[h * tokens : (h + 1) * tokens]
+    def attention():
+        lax.fori_loop(1, me + 1, share, 0)
+        top, total, summed = lax.fori_loop(
+            0,
+            me + 1,
+            attend,
+            (jnp.full((rows, 1), -1e30, F32), jnp.zeros((rows, 1), F32), jnp.zeros((rows, HD), F32)),
+        )
+        attended = (summed / total).astype(BF16)
+        for h in range(heads_here):
+            both[:, channels + h * HD : channels + (h + 1) * HD] = attended[h * tokens : (h + 1) * tokens]
+
+    pl.when(me >= n_seq // 2)(attention)
 
     @pl.when(pair == 0)
     def _():
@@ -408,6 +415,7 @@
     through[1:2, :] = jnp.where(
         seg_second == seg_first, jnp.exp(dot(meta[second, 0:1, 0:heads], spread, (1, 0), HIGHEST)), 0.0
     )
+    through[2:3, :] = gain_ref[...].reshape(1, channels)
     c_copy().wait_recv()
     on_left = side == 0
     for c in range(chunks):
@@ -432,23 +440,23 @@
         theirs = jnp.where(on_left, enter_second, enter_first).astype(BF16)
         f_send[c] = dot(partner_c[...], theirs, (1, 0)).astype(BF16)
         hop(f_send, f_recv, f_ss, f_rs, c, partner).start()
-        ours = jnp.where(on_left, enter_first, enter_second).astype(BF16)
-        carried_ref[:, cols] = dot(read_c, ours, (1, 0))
-
-    for c in range(chunks):
-        hop(f_send, f_recv, f_ss, f_rs, c, partner).wait_recv()
-        carried_ref[:, part(1 - side, c)] = f_recv[c].astype(F32)
+        entering[c] = jnp.where(on_left, enter_first, enter_second).astype(BF16)
 
     joined = segs_col == prev_last
-    gain_row = gain_ref[...].reshape(1, channels)
     same_head = (iota((LANES, LANES), 0) // HEAD_CHANNELS == iota((LANES, LANES), 1) // HEAD_CHANNELS).astype(F32)
-    for p in range(pairs):
-        cols = slice(p * LANES, (p + 1) * LANES)
-        carried = carried_ref[:, cols]
+
+    def norm(cols, carried):
         y = y_ref[:, cols] + jnp.where(joined, jnp.exp(cumx[:, cols]), 0.0) * carried
         gated = y * jax.nn.silu(gate_ref[:, cols].astype(F32))
         mean_square = dot(gated * gated, same_head, (1, 0), HIGHEST) * (1.0 / HEAD_CHANNELS)
-        both[:, cols] = (gated * lax.rsqrt(mean_square + 1e-05) * gain_row[:, cols]).astype(BF16)
+        both[:, cols] = (gated * lax.rsqrt(mean_square + 1e-05) * through[2:3, cols]).astype(BF16)
+
+    pl.when(me < n_seq // 2)(attention)
+    for c in range(chunks):
+        norm(part(side, c), dot(read_c, entering[c], (1, 0)))
+    for c in range(chunks):
+        hop(f_send, f_recv, f_ss, f_rs, c, partner).wait_recv()
+        norm(part(1 - side, c), f_recv[c].astype(F32))
 
     for w in weights:
         w.wait()
@@ -539,7 +547,7 @@
         *[pltpu.VMEM(hops, BF16) for _ in range(4)],
         *[pltpu.VMEM((chunks, tokens, LANES), BF16) for _ in range(2)],
         pltpu.VMEM((tokens, STATE_SIZE), BF16),
-        pltpu.VMEM((tokens, channels), F32),
+        pltpu.VMEM(hops, BF16),
         pltpu.VMEM((8, channels), F32),
         pltpu.VMEM((tokens, channels + query.shape[1]), BF16),
         pltpu.VMEM((n_head - 1, tokens, out_width), BF16),
@@ -566,7 +574,7 @@
         out_specs=vmem,
         scratch_shapes=scratch,
         compiler_params=pltpu.CompilerParams(
-            collective_id=0, has_side_effects=True, vmem_limit_bytes=48 * 2**20
+            collective_id=0, has_side_effects=True, vmem_limit_bytes=64 * 2**20
         ),
         name="mixer",
     )(

time: 52 us -> 38.2 us (0.73)
  local copies, waits for them, and re-layouts: 13.8 us -> 1.57 us
  Pallas kernels: 37.6 us -> 35.9 us
    unnamed x31 -> x1, local copies, waits for them, and re-layouts: 13.8 us -> 1.57 us
    pallas_call x1, Pallas kernels: 37.6 us -> 35.9 us  [shards(): pl.pallas_call(functools.partial(kernel, n_seq, n_head), out_shape=jax.Sh...]
where the time goes in v3:
time: 38.2 us; the launch traced here: 37.5 us
  Pallas kernels  35.9 us (94%)
  local copies, waits for them, and re-layouts  1.57 us (4%)
    pallas_call x1, Pallas kernels, shards(): pl.pallas_call(functools.partial(kernel, n_seq, n_head), out_shape=jax.Sh...  35.9 us
    unnamed x1, local copies, waits for them, and re-layouts  1.57 us

profile of v3, /device:TPU:25, one launch (start us, length us, event | category | flops | bytes accessed | tf_op | source)
XLA Modules:
  0.0 37.5 jit_solution(660257204600327187)
XLA Ops:
  0.0 35.9 %mixer.1 = bf16[128,512]{1,0:T(8,128)(2,1)} custom-call(bf16[128,768]{1,0:T(8,128)(2,1)} %inner_hbm.1, bf16[128,512]{1,0:T(8,128)(2,1)} %groups_hbm.1, bf16[128,768]{1,0:T(8,128)(2,1)} %gate_hbm.1, f32[12,128]{1,0:T(8,128)} %step_hbm.1, f32[12]{0:T(128)} %bias_hbm.1, f32[12]{0:T(128)} %decay_hbm.1, f32[4,768]{1,0:T(4,128)} %taps_inner_hbm.1, ...), custom_call_target="tpu_custom_call" | custom-call | tf_op jit(solution)/shard_map/mixer/pallas_call | solution.py:570
  35.9 1.6 %copy.17 = bf16[128,512]{1,0:T(8,128)(2,1)} copy(bf16[128,512]{1,0:T(8,128)(2,1)} %mixer.1) | data formatting | bytes 262144

commit v4 on v3

--- a/solution.py
+++ b/solution.py
@@ -318,9 +318,11 @@
             src.at[c], dst.at[c], ss.at[c], rs.at[c], device_id=at_seq(target), device_id_type=MESH
         )
 
-    for c in range(chunks):
-        s_send[c] = state[:, part(1 - side, c)].astype(BF16)
-        hop(s_send, s_recv, s_ss, s_rs, c, partner).start()
+    depth = STATE_SIZE // 2
+    for i in range(2 * chunks):
+        c, r = i // 2, i % 2
+        s_send[i] = state[r * depth : (r + 1) * depth, part(1 - side, c)].astype(BF16)
+        hop(s_send, s_recv, s_ss, s_rs, i, partner).start()
 
     def c_copy():
         return pltpu.make_async_remote_copy(
@@ -422,25 +424,29 @@
         cols = part(side, c)
         through_first = through[0:1, cols]
         through_second = through[1:2, cols]
-        hop(s_send, s_recv, s_ss, s_rs, c, partner).wait_recv()
-        own, others = state[:, cols], s_recv[c].astype(F32)
-
-        @pl.when(pair > 0)
-        def _():
-            hop(e_send, e_recv, e_ss, e_rs, c, lower).wait_recv()
-
-        enter_first = e_recv[c].astype(F32)
-        enter_second = through_first * enter_first + jnp.where(on_left, own, others)
-
-        @pl.when(pair < last_pair)
-        def _():
-            e_send[c] = (through_second * enter_second + jnp.where(on_left, others, own)).astype(BF16)
-            hop(e_send, e_recv, e_ss, e_rs, c, upper).start()
-
-        theirs = jnp.where(on_left, enter_second, enter_first).astype(BF16)
-        f_send[c] = dot(partner_c[...], theirs, (1, 0)).astype(BF16)
+        theirs = []
+        for r in range(2):
+            i, span = 2 * c + r, slice(r * depth, (r + 1) * depth)
+            hop(s_send, s_recv, s_ss, s_rs, i, partner).wait_recv()
+            own, others = state[span, cols], s_recv[i].astype(F32)
+
+            @pl.when(pair > 0)
+            def _():
+                hop(e_send, e_recv, e_ss, e_rs, i, lower).wait_recv()
+
+            enter_first = e_recv[i].astype(F32)
+            enter_second = through_first * enter_first + jnp.where(on_left, own, others)
+
+            @pl.when(pair < last_pair)
+            def _():
+                e_send[i] = (through_second * enter_second + jnp.where(on_left, others, own)).astype(BF16)
+                hop(e_send, e_recv, e_ss, e_rs, i, upper).start()
+
+            theirs.append(jnp.where(on_left, enter_second, enter_first).astype(BF16))
+            entering[c, span, :] = jnp.where(on_left, enter_first, enter_second).astype(BF16)
+
+        f_send[c] = dot(partner_c[...], jnp.concatenate(theirs, axis=0), (1, 0)).astype(BF16)
         hop(f_send, f_recv, f_ss, f_rs, c, partner).start()
-        entering[c] = jnp.where(on_left, enter_first, enter_second).astype(BF16)
 
     joined = segs_col == prev_last
     same_head = (iota((LANES, LANES), 0) // HEAD_CHANNELS == iota((LANES, LANES), 1) // HEAD_CHANNELS).astype(F32)
@@ -462,8 +468,8 @@
         w.wait()
     width = out_ref.shape[1]
 
-    def product(j):
-        cols = pl.ds(pl.multiple_of(j * width, LANES), width)
+    def product(j, part_of):
+        cols = pl.ds(pl.multiple_of(j * width + part_of * (width // 2), LANES), width // 2)
         return dot(both[:, :channels], mproj[:, cols], (1, 0)) + dot(both[:, channels:], aproj[:, cols], (1, 0))
 
     def rs_copy(i, target):
@@ -471,22 +477,28 @@
             rs_send.at[i], rs_recv.at[i], rs_ss.at[i], rs_rs.at[i], device_id=at_head(target), device_id_type=MESH
         )
 
-    to_pair, to_sibling, to_opposite = rs_copy(0, sibling), rs_copy(1, sibling), rs_copy(2, opposite)
-    rs_send[0] = product(opposite_sibling).astype(BF16)
-    to_pair.start()
-    rs_send[1] = product(sibling).astype(BF16)
-    to_sibling.start()
-    away = product(opposite)
-    to_pair.wait_recv()
-    rs_send[2] = (away + rs_recv[0].astype(F32)).astype(BF16)
-    to_opposite.start()
-    result = product(mine)
-    to_sibling.wait_recv()
-    result = result + rs_recv[1].astype(F32)
-    to_opposite.wait_recv()
-    out_ref[...] = (result + rs_recv[2].astype(F32)).astype(BF16)
-
-    for copy in (to_pair, to_sibling, to_opposite, c_copy()):
+    to_pair = [rs_copy(h, sibling) for h in range(2)]
+    to_sibling = [rs_copy(2 + h, sibling) for h in range(2)]
+    to_opposite = [rs_copy(4 + h, opposite) for h in range(2)]
+    for h in range(2):
+        rs_send[h] = product(opposite_sibling, h).astype(BF16)
+        to_pair[h].start()
+    for h in range(2):
+        away = product(opposite, h)
+        to_pair[h].wait_recv()
+        rs_send[4 + h] = (away + rs_recv[h].astype(F32)).astype(BF16)
+        to_opposite[h].start()
+    for h in range(2):
+        rs_send[2 + h] = product(sibling, h).astype(BF16)
+        to_sibling[h].start()
+    for h in range(2):
+        result = product(mine, h)
+        to_sibling[h].wait_recv()
+        result = result + rs_recv[2 + h].astype(F32)
+        to_opposite[h].wait_recv()
+        out_ref[:, h * (width // 2) : (h + 1) * (width // 2)] = (result + rs_recv[4 + h].astype(F32)).astype(BF16)
+
+    for copy in (*to_pair, *to_sibling, *to_opposite, c_copy()):
         copy.wait_send()
 
     def sent_share(d, _):
@@ -512,12 +524,13 @@
 
     lax.fori_loop(me + 1, n_seq, sent_kv, 0)
     for c in range(chunks):
-        hop(s_send, s_recv, s_ss, s_rs, c, partner).wait_send()
         hop(f_send, f_recv, f_ss, f_rs, c, partner).wait_send()
+    for i in range(2 * chunks):
+        hop(s_send, s_recv, s_ss, s_rs, i, partner).wait_send()
 
         @pl.when(pair < last_pair)
         def _():
-            hop(e_send, e_recv, e_ss, e_rs, c, upper).wait_send()
+            hop(e_send, e_recv, e_ss, e_rs, i, upper).wait_send()
 
 
 def shards(n_seq, n_head, *arrays):
@@ -544,14 +557,14 @@
         pltpu.VMEM((tokens, channels), F32),
         pltpu.VMEM((tokens, channels), F32),
         pltpu.VMEM((STATE_SIZE, channels), F32),
-        *[pltpu.VMEM(hops, BF16) for _ in range(4)],
+        *[pltpu.VMEM((2 * chunks, STATE_SIZE // 2, LANES), BF16) for _ in range(4)],
         *[pltpu.VMEM((chunks, tokens, LANES), BF16) for _ in range(2)],
         pltpu.VMEM((tokens, STATE_SIZE), BF16),
         pltpu.VMEM(hops, BF16),
         pltpu.VMEM((8, channels), F32),
         pltpu.VMEM((tokens, channels + query.shape[1]), BF16),
-        pltpu.VMEM((n_head - 1, tokens, out_width), BF16),
-        pltpu.VMEM((n_head - 1, tokens, out_width), BF16),
+        pltpu.VMEM((6, tokens, out_width // 2), BF16),
+        pltpu.VMEM((6, tokens, out_width // 2), BF16),
         dma((13,)),
         dma((2,)),
         dma((2, 2)),
@@ -563,9 +576,10 @@
         dma((n_seq,)),
         dma((1,)),
         dma((1,)),
-        *[dma((chunks,)) for _ in range(6)],
-        dma((n_head - 1,)),
-        dma((n_head - 1,)),
+        *[dma((2 * chunks,)) for _ in range(4)],
+        *[dma((chunks,)) for _ in range(2)],
+        dma((6,)),
+        dma((6,)),
     ]
     return pl.pallas_call(
         functools.partial(kernel, n_seq, n_head),

time: 38.2 us -> 37.4 us (0.979)
  Pallas kernels: 35.9 us -> 35.1 us
    pallas_call x1, Pallas kernels: 35.9 us -> 35.1 us  [shards(): pl.pallas_call(functools.partial(kernel, n_seq, n_head), out_shape=jax.Sh...]
where the time goes in v4:
time: 37.4 us; the launch traced here: 36.7 us
  Pallas kernels  35.1 us (94%)
  local copies, waits for them, and re-layouts  1.57 us (4%)
    pallas_call x1, Pallas kernels, shards(): pl.pallas_call(functools.partial(kernel, n_seq, n_head), out_shape=jax.Sh...  35.1 us
    unnamed x1, local copies, waits for them, and re-layouts  1.57 us

profile of v4, /device:TPU:25, one launch (start us, length us, event | category | flops | bytes accessed | tf_op | source)
XLA Modules:
  0.0 36.7 jit_solution(4367709395797226314)
XLA Ops:
  0.0 35.1 %mixer.1 = bf16[128,512]{1,0:T(8,128)(2,1)} custom-call(bf16[128,768]{1,0:T(8,128)(2,1)} %inner_hbm.1, bf16[128,512]{1,0:T(8,128)(2,1)} %groups_hbm.1, bf16[128,768]{1,0:T(8,128)(2,1)} %gate_hbm.1, f32[12,128]{1,0:T(8,128)} %step_hbm.1, f32[12]{0:T(128)} %bias_hbm.1, f32[12]{0:T(128)} %decay_hbm.1, f32[4,768]{1,0:T(4,128)} %taps_inner_hbm.1, ...), custom_call_target="tpu_custom_call" | custom-call | tf_op jit(solution)/shard_map/mixer/pallas_call | solution.py:584
  35.2 1.6 %copy.17 = bf16[128,512]{1,0:T(8,128)(2,1)} copy(bf16[128,512]{1,0:T(8,128)(2,1)} %mixer.1) | data formatting | bytes 262144
